TPU v7x, 32 devices: a whole 2x2x4 slice. The times are simulated.
32 devices in a mesh: space: 8 (over z, x), group: 4 (over y, core).
Axes of the slice: x: 2, y: 2, z: 4, core: 2. Of those that a mesh axis runs over, the one named last changes fastest.
Arguments:
- point_feats: bfloat16 [32768, 32], P(('space', 'group')), may hold values from -6 to 6
- point_voxel: int32 [32768], P(('space', 'group')), may hold values from -1 to 4095, as said below
- cotangent: bfloat16 [32768, 32], P(('space', 'group')), may hold values from -6 to 6
- kernel: bfloat16 [3, 3, 3, 32, 32], replicated, may hold values from -0.21875 to 0.21875
Outputs:
- point_grad: bfloat16 [32768, 32], P(('space', 'group'))
Inputs may be any that keep to these rules, and one draw needn't show every extreme that they name: `point_voxel`: in each block of 256 slots that one device sends to one member of its group the live slots come first and hold voxel numbers below 4096, the rest -1; every device fills one of its blocks completely.
All inputs are finite; a program needn't handle non-finite values.
Results may differ from a plain program's by a relative error of at most 0.0049.
Values may be sent and summed in bfloat16 or wider, within the bound.
A program may use at most 64 MiB of HBM per device.

v0:
```python
import jax
import jax.numpy as jnp
from jax import lax
from jax.sharding import PartitionSpec as P

XD = 16
YD = 16
ZB = 16


def extended(shard, sides, width):
    for axis, dim in sides:
        size, length = (lax.axis_size(axis), shard.shape[dim])
        up = [(i, (i + 1) % size) for i in range(size - 1)]
        down = [(j, i) for i, j in up]
        last = lax.slice_in_dim(shard, length - width, length, axis=dim)
        first = lax.slice_in_dim(shard, 0, width, axis=dim)
        before = lax.ppermute(last, axis, up)
        after = lax.ppermute(first, axis, down)
        shard = jnp.concatenate([before, shard, after], axis=dim)
    return shard


def convolve(padded, weights):
    return lax.conv_general_dilated(
        padded[None],
        weights,
        (1, 1, 1),
        "VALID",
        dimension_numbers=("NDHWC", "DHWIO", "NDHWC"),
        preferred_element_type=jnp.float32,
    )[0]


def pad_depth(field):
    return jnp.pad(field, ((0, 0), (0, 0), (1, 1), (0, 0)))


def forward_conv(padded, kernel):
    return convolve(padded, kernel)


def per_device(point_feats, point_voxel, cotangent, kernel):
    voxels = XD * YD * ZB
    channels = point_feats.shape[1]
    feats_in, cot_in, voxel_in = (
        lax.all_to_all(point_feats, "group", split_axis=0, concat_axis=0, tiled=True),
        lax.all_to_all(cotangent, "group", split_axis=0, concat_axis=0, tiled=True),
        lax.all_to_all(point_voxel, "group", split_axis=0, concat_axis=0, tiled=True),
    )
    index = jnp.where(voxel_in >= 0, voxel_in, voxels).astype(jnp.int32)
    sums = jax.ops.segment_sum(feats_in.astype(jnp.float32), index, voxels + 1)
    counts = jax.ops.segment_sum(jnp.ones(index.shape, jnp.float32), index, voxels + 1)
    divisor = jnp.maximum(counts, 1.0)
    mean = (sums / divisor[:, None])[:voxels].reshape(XD, YD, ZB, channels).astype(jnp.bfloat16)
    flipped = jnp.swapaxes(kernel[::-1, ::-1, ::-1], 3, 4)
    padded = pad_depth(extended(mean, (("space", 0), ("group", 1)), 1))
    out = forward_conv(padded, kernel)
    gy = jax.ops.segment_sum(cot_in.astype(jnp.float32), index, voxels + 1)[:voxels].reshape(
        XD, YD, ZB, channels
    )
    sig = jax.nn.sigmoid(out)
    gout = (gy * sig * (1.0 + out * (1.0 - sig))).astype(jnp.bfloat16)
    grad_padded = pad_depth(extended(gout, (("space", 0), ("group", 1)), 1))
    ggrid = convolve(grad_padded, flipped)
    table = jnp.concatenate(
        [ggrid.reshape(voxels, channels), jnp.zeros((1, channels), jnp.float32)], axis=0
    )
    grads = (table[index] / divisor[index][:, None]).astype(jnp.bfloat16)
    return lax.all_to_all(grads, "group", split_axis=0, concat_axis=0, tiled=True)


def solution(mesh):
    placed = (P(("space", "group"), None), P(("space", "group")), P(("space", "group"), None), P())
    return jax.shard_map(
        per_device,
        mesh=mesh,
        in_specs=placed,
        out_specs=P(("space", "group"), None),
        check_vma=False,
    )
```

profile of v0, /device:TPU:0, one launch (start us, length us, event | category | flops | bytes accessed | tf_op | source)
XLA Modules:
  0.0 114.0 jit_solution(4955369461226787972)
XLA Ops:
  0.0 4.4 %all-to-all-start = ((s32[4,256,1]{1,2,0:T(1,128)}), s32[4,256,1]{1,2,0:T(1,128)S(1)}, u32[]{:S(2)}, u32[]{:S(2)}) async-start(s32[4,256,1]{1,2,0:T(1,128)} %bitcast.69), calls=%async_computation | async-start | bytes 8192 | tf_op jit(solution)/shard_map/all_to_all | solution.py:49
  4.4 1.5 %copy.63 = bf16[4,4,8,256]{3,2,0,1:T(8,128)(2,1)} copy(bf16[4,4,8,256]{3,2,1,0:T(8,128)(2,1)} %bitcast.60) | data formatting | bytes 131072 | tf_op jit(solution)/shard_map/all_to_all | solution.py:47
  5.8 2.3 %all-to-all-done = s32[4,256,1]{1,2,0:T(1,128)S(1)} async-done(((s32[4,256,1]{1,2,0:T(1,128)}), s32[4,256,1]{1,2,0:T(1,128)S(1)}, u32[]{:S(2)}, u32[]{:S(2)}) %all-to-all-start) | async-done | bytes 4128 | tf_op jit(solution)/shard_map/all_to_all | solution.py:49
  8.2 3.3 %all-to-all-start.2 = ((bf16[4,256,32]{1,2,0:T(8,128)(2,1)}), bf16[4,256,32]{1,2,0:T(8,128)(2,1)S(1)}, u32[]{:S(2)}, u32[]{:S(2)}) async-start(bf16[4,256,32]{1,2,0:T(8,128)(2,1)} %bitcast.47), calls=%async_computation.2 | async-start | bytes 131072 | tf_op jit(solution)/shard_map/all_to_all | solution.py:47
  11.5 6.8 %scatter_custom_fusion.2 = f32[4097]{0:T(1024)S(1)} fusion(s32[1024]{0:T(1024)S(1)} %bitcast.66, f32[1024]{0:T(1024)S(1)} %broadcast.65, f32[]{:T(128)} %constant.6.clone.1), kind=kCustom, calls=%fused_computation.67 | custom fusion | flops 1024 | bytes 16392 | tf_op jit(solution)/shard_map/scatter-add | solution.py:53
  18.4 7.2 %scatter_custom_fusion.1 = f32[4097,32]{1,0:T(8,128)S(1)} fusion(s32[1024]{0:T(1024)S(1)} %bitcast.67, f32[1024,32]{1,0:T(8,128)S(1)} %bitcast.58, f32[]{:T(128)} %constant.6.clone.1), kind=kCustom, calls=%fused_computation.51 | custom fusion | flops 32768 | bytes 524420 | tf_op jit(solution)/shard_map/scatter-add | solution.py:52
  25.7 1.8 %divide_convert_fusion = bf16[4097,32]{1,0:T(8,128)(2,1)S(1)} fusion(f32[4097,32]{1,0:T(8,128)S(1)} %scatter_custom_fusion.1, f32[4097]{0:T(1024)S(1)} %broadcast_maximum_fusion), kind=kLoop, calls=%fused_computation.26 | loop fusion | flops 262208 | bytes 803012 | tf_op jit(solution)/shard_map/convert.2
  27.5 1.3 %collective-permute-start.1 = (bf16[1,16,16,32]{3,2,1,0:T(8,128)(2,1)S(1)}, bf16[1,16,16,32]{3,2,1,0:T(8,128)(2,1)S(1)}, u32[]{:S(2)}, u32[]{:S(2)}) collective-permute-start(bf16[1,16,16,32]{3,2,1,0:T(8,128)(2,1)S(1)} %bitcast.63), channel_id=1, source_target_pairs={{4,0},{8,4},{12,8},{16,12},{20,16},{24,20},{28,24},{5,1},{9,5},{13... | collective-permute-start | bytes 49160 | tf_op jit(solution)/shard_map/ppermute | solution.py:19
  28.8 4.5 %collective-permute-start = (bf16[1,16,16,32]{3,2,1,0:T(8,128)(2,1)S(1)}, bf16[1,16,16,32]{3,2,1,0:T(8,128)(2,1)S(1)}, u32[]{:S(2)}, u32[]{:S(2)}) collective-permute-start(bf16[1,16,16,32]{3,2,1,0:T(8,128)(2,1)S(1)} %bitcast.62), channel_id=1, source_target_pairs={{0,4},{4,8},{8,12},{12,16},{16,20},{20,24},{24,28},{1,5},{5,9},{9,... | collective-permute-start | bytes 49160 | tf_op jit(solution)/shard_map/ppermute | solution.py:18
  34.0 3.6 %all-to-all-start.1 = ((bf16[4,256,32]{1,2,0:T(8,128)(2,1)}), bf16[4,256,32]{1,2,0:T(8,128)(2,1)S(1)}, u32[]{:S(2)}, u32[]{:S(2)}) async-start(bf16[4,256,32]{1,2,0:T(8,128)(2,1)} %bitcast.48), calls=%async_computation.1 | async-start | bytes 131072 | tf_op jit(solution)/shard_map/all_to_all | solution.py:48
  37.7 0.7 pad_maximum_fusion.5
  38.4 3.0 %collective-permute-start.2 = (bf16[18,1,16,32]{3,2,1,0:T(8,128)(2,1)}, bf16[18,1,16,32]{3,2,1,0:T(8,128)(2,1)}, u32[]{:S(2)}, u32[]{:S(2)}) collective-permute-start(bf16[18,1,16,32]{3,2,1,0:T(8,128)(2,1)} %get-tuple-element.7), channel_id=1, source_target_pairs={{0,1},{1,2},{2,3},{4,5},{5,6},{6,7},{8,9},{9,10},{10,11},{12,13},{... | collective-permute-start | bytes 55304 | tf_op jit(solution)/shard_map/ppermute | solution.py:18
  41.4 1.3 %collective-permute-start.3 = (bf16[18,1,16,32]{3,2,1,0:T(8,128)(2,1)}, bf16[18,1,16,32]{3,2,1,0:T(8,128)(2,1)}, u32[]{:S(2)}, u32[]{:S(2)}) collective-permute-start(bf16[18,1,16,32]{3,2,1,0:T(8,128)(2,1)} %get-tuple-element.8), channel_id=1, source_target_pairs={{1,0},{2,1},{3,2},{5,4},{6,5},{7,6},{9,8},{10,9},{11,10},{13,12},{... | collective-permute-start | bytes 55304 | tf_op jit(solution)/shard_map/ppermute | solution.py:19
  42.7 0.9 copy.47
  43.7 7.8 %scatter_custom_fusion = f32[4097,32]{1,0:T(8,128)S(1)} fusion(s32[1024]{0:T(1024)S(1)} %bitcast.68, f32[1024,32]{1,0:T(8,128)} %bitcast.57, f32[]{:T(128)} %constant.6.clone.1), kind=kCustom, calls=%fused_computation.53 | custom fusion | flops 32768 | bytes 524928 | tf_op jit(solution)/shard_map/scatter-add | solution.py:59
  51.5 2.6 %fusion.26 = bf16[18,18,1,18,32]{4,3,1,0,2:T(8,128)(2,1)S(1)} fusion(bf16[18,1,16,32]{3,2,1,0:T(8,128)(2,1)} %collective-permute-done.3, bf16[18,1,16,32]{3,2,1,0:T(8,128)(2,1)} %collective-permute-done.2, bf16[1,16,16,32]{3,2,1,0:T(8,128)(2,1)S(1)} %collective-permute-done.1, bf16[16,16,16,32]{3,2,1,0:T(8,128)(2,1)S(1)} %bitcast.51, ...), kind=kLoop, calls=%fused_computation.40 | loop fusion | flops 3359232 | bytes 705024 | tf_op jit(solution)/shard_map/broadcast_in_dim | solution.py:26
  54.2 1.7 %pad.10 = bf16[18,18,1,24,32]{4,3,1,0,2:T(8,128)(2,1)} pad(bf16[18,18,1,18,32]{4,3,1,0,2:T(8,128)(2,1)S(1)} %fusion.26, bf16[]{:T(256)} %constant.1.clone.1), padding=0_0x0_0x0_0x0_6x0_0 | pad | bytes 870914 | tf_op jit(solution)/shard_map/broadcast_in_dim | solution.py:26
  55.9 5.1 %reshape.65 = bf16[18,18,1,8,3,32]{5,4,3,1,0,2:T(4,128)(2,1)S(1)} reshape(bf16[18,18,1,24,32]{4,3,1,0,2:T(8,128)(2,1)} %pad.10) | data formatting | bytes 995328 | tf_op jit(solution)/shard_map/conv_general_dilated | solution.py:25
  62.0 4.6 %fusion.35 = f32[16,16,8,3,32]{4,2,3,1,0:T(8,128)S(1)} fusion(bf16[3,3,3,32,32]{4,3,2,1,0:T(8,128)(2,1)S(1)} %copy-done, bf16[18,18,1,7,2,32]{5,3,4,1,0,2:T(8,128)(2,1)S(1)} %slice.63, bf16[18,18,1,8,3,32]{5,3,4,1,0,2:T(8,128)(2,1)S(1)} %copy.37, pred[8,3]{0,1:T(4,128)(4,1)S(1)} %copy-done.3), kind=kOutput, calls=%fused_computation.48 | convolution fusion | flops 342423552 | bytes 1629720 | tf_op jit(solution)/shard_map/conv_general_dilated | solution.py:25
  67.2 1.0 slice-done
  68.2 1.1 fusion.19
  69.3 4.4 %collective-permute-start.4 = (bf16[1,16,16,32]{3,1,2,0:T(8,128)(2,1)S(1)}, bf16[1,16,16,32]{3,1,2,0:T(8,128)(2,1)S(1)}, u32[]{:S(2)}, u32[]{:S(2)}) collective-permute-start(bf16[1,16,16,32]{3,1,2,0:T(8,128)(2,1)S(1)} %get-tuple-element.11), channel_id=1, source_target_pairs={{0,4},{4,8},{8,12},{12,16},{16,20},{20,24},{24,28},{1,5},{5,9},{9,... | collective-permute-start | bytes 49160 | tf_op jit(solution)/shard_map/ppermute | solution.py:18
  73.8 1.3 %collective-permute-start.5 = (bf16[1,16,16,32]{3,1,2,0:T(8,128)(2,1)S(1)}, bf16[1,16,16,32]{3,1,2,0:T(8,128)(2,1)S(1)}, u32[]{:S(2)}, u32[]{:S(2)}) collective-permute-start(bf16[1,16,16,32]{3,1,2,0:T(8,128)(2,1)S(1)} %get-tuple-element.12), channel_id=1, source_target_pairs={{4,0},{8,4},{12,8},{16,12},{20,16},{24,20},{28,24},{5,1},{9,5},{13... | collective-permute-start | bytes 49160 | tf_op jit(solution)/shard_map/ppermute | solution.py:19
  75.1 0.9 collective-permute-done.4
  76.0 4.6 %collective-permute-done.5 = bf16[1,16,16,32]{3,1,2,0:T(8,128)(2,1)S(1)} collective-permute-done((bf16[1,16,16,32]{3,1,2,0:T(8,128)(2,1)S(1)}, bf16[1,16,16,32]{3,1,2,0:T(8,128)(2,1)S(1)}, u32[]{:S(2)}, u32[]{:S(2)}) %collective-permute-start.5) | collective-permute-done | bytes 16416 | tf_op jit(solution)/shard_map/ppermute | solution.py:19
  80.9 2.0 %collective-permute-start.6 = (bf16[18,1,16,32]{3,1,2,0:T(2,128)(2,1)S(1)}, bf16[18,1,16,32]{3,1,2,0:T(2,128)(2,1)S(1)}, u32[]{:S(2)}, u32[]{:S(2)}) collective-permute-start(bf16[18,1,16,32]{3,1,2,0:T(2,128)(2,1)S(1)} %get-tuple-element.5), channel_id=1, source_target_pairs={{0,1},{1,2},{2,3},{4,5},{5,6},{6,7},{8,9},{9,10},{10,11},{12,13},{... | collective-permute-start | bytes 55304 | tf_op jit(solution)/shard_map/ppermute | solution.py:18
  83.0 1.5 %collective-permute-start.7 = (bf16[18,1,16,32]{3,1,2,0:T(2,128)(2,1)S(1)}, bf16[18,1,16,32]{3,1,2,0:T(2,128)(2,1)S(1)}, u32[]{:S(2)}, u32[]{:S(2)}) collective-permute-start(bf16[18,1,16,32]{3,1,2,0:T(2,128)(2,1)S(1)} %get-tuple-element.6), channel_id=1, source_target_pairs={{1,0},{2,1},{3,2},{5,4},{6,5},{7,6},{9,8},{10,9},{11,10},{13,12},{... | collective-permute-start | bytes 55304 | tf_op jit(solution)/shard_map/ppermute | solution.py:19
  84.5 6.2 %gather_fusion.1 = f32[1024]{0:T(1024)S(1)} fusion(f32[4097]{0:T(1024)S(1)} %broadcast_maximum_fusion, s32[1024]{0:T(1024)S(1)} %broadcast_clamp_fusion), kind=kCustom, calls=%fused_computation.1 | custom fusion | bytes 12288 | tf_op jit(solution)/shard_map/gather | solution.py:69
  90.7 2.1 %fusion.20 = bf16[18,18,1,18,32]{4,1,3,0,2:T(8,128)(2,1)S(1)} fusion(bf16[18,1,16,32]{3,1,2,0:T(2,128)(2,1)S(1)} %collective-permute-done.7, bf16[18,1,16,32]{3,1,2,0:T(2,128)(2,1)S(1)} %collective-permute-done.6, bf16[1,16,16,32]{3,1,2,0:T(8,128)(2,1)S(1)} %collective-permute-done.5, bf16[16,16,16,32]{3,1,2,0:T(8,128)(2,1)S(1)} %fusion.19, ...), kind=kLoop, calls=%fused_computation.32 | loop fusion | flops 3359232 | bytes 705024 | tf_op jit(solution)/shard_map/broadcast_in_dim | solution.py:26
  94.1 4.6 %fusion.32 = f32[16,16,8,3,32]{4,2,3,1,0:T(8,128)S(1)} fusion(bf16[3,3,3,32,32]{4,3,2,1,0:T(8,128)(2,1)S(1)} %copy-done, bf16[18,18,1,7,2,32]{5,3,4,1,0,2:T(8,128)(2,1)S(1)} %slice.67, bf16[18,18,1,8,3,32]{5,3,4,1,0,2:T(8,128)(2,1)S(1)} %copy.42, pred[8,3]{0,1:T(4,128)(4,1)S(1)} %copy-done.3), kind=kOutput, calls=%fused_computation.47 | convolution fusion | flops 342423552 | bytes 1629720 | tf_op jit(solution)/shard_map/conv_general_dilated | solution.py:25
  100.3 2.8 %gather_fusion = f32[1024,32]{1,0:T(8,128)S(1)} fusion(f32[4097,32]{1,0:T(8,128)S(1)} %concatenate.19, s32[1024]{0:T(1024)S(1)} %broadcast_clamp_fusion), kind=kCustom, calls=%fused_computation | custom fusion | bytes 266240 | tf_op jit(solution)/shard_map/gather | solution.py:69
  103.3 10.1 %all_to_all.39 = bf16[4,256,32]{1,2,0:T(8,128)(2,1)S(1)} all-to-all(bf16[4,256,32]{1,2,0:T(8,128)(2,1)S(1)} %divide_convert_fusion.1), channel_id=1, replica_groups=mesh['space'=8,'group'=4] {'group'}, dimensions={0} | all-to-all | bytes 131072 | tf_op jit(solution)/shard_map/all_to_all | solution.py:70
  (41 shorter events, 6.4 us)
Async XLA Ops:
  0.0 61.7 %copy-start = (bf16[3,3,3,32,32]{4,3,2,1,0:T(8,128)(2,1)S(1)}, bf16[3,3,3,32,32]{4,3,2,1,0:T(8,128)(2,1)}, u32[]{:S(2)}) copy-start(bf16[3,3,3,32,32]{4,3,2,1,0:T(8,128)(2,1)} %param.7) | copy-start | bytes 165892
  0.0 8.2 %all-to-all-start = ((s32[4,256,1]{1,2,0:T(1,128)}), s32[4,256,1]{1,2,0:T(1,128)S(1)}, u32[]{:S(2)}, u32[]{:S(2)}) async-start(s32[4,256,1]{1,2,0:T(1,128)} %bitcast.69), calls=%async_computation | async-start | bytes 8192 | tf_op jit(solution)/shard_map/all_to_all | solution.py:49
  8.2 10.1 %all-to-all-start.2 = ((bf16[4,256,32]{1,2,0:T(8,128)(2,1)}), bf16[4,256,32]{1,2,0:T(8,128)(2,1)S(1)}, u32[]{:S(2)}, u32[]{:S(2)}) async-start(bf16[4,256,32]{1,2,0:T(8,128)(2,1)} %bitcast.47), calls=%async_computation.2 | async-start | bytes 131072 | tf_op jit(solution)/shard_map/all_to_all | solution.py:47
  25.6 7.7 %copy-start.2 = (bf16[1024,32]{0,1:T(8,128)(2,1)S(1)}, bf16[1024,32]{0,1:T(8,128)(2,1)}, u32[]{:S(2)}) copy-start(bf16[1024,32]{0,1:T(8,128)(2,1)} %param.6) | copy-start | bytes 196612
  27.5 10.2 %collective-permute-start.1 = (bf16[1,16,16,32]{3,2,1,0:T(8,128)(2,1)S(1)}, bf16[1,16,16,32]{3,2,1,0:T(8,128)(2,1)S(1)}, u32[]{:S(2)}, u32[]{:S(2)}) collective-permute-start(bf16[1,16,16,32]{3,2,1,0:T(8,128)(2,1)S(1)} %bitcast.63), channel_id=1, source_target_pairs={{4,0},{8,4},{12,8},{16,12},{20,16},{24,20},{28,24},{5,1},{9,5},{13... | collective-permute-start | bytes 49160 | tf_op jit(solution)/shard_map/ppermute | solution.py:19
  28.8 8.9 %collective-permute-start = (bf16[1,16,16,32]{3,2,1,0:T(8,128)(2,1)S(1)}, bf16[1,16,16,32]{3,2,1,0:T(8,128)(2,1)S(1)}, u32[]{:S(2)}, u32[]{:S(2)}) collective-permute-start(bf16[1,16,16,32]{3,2,1,0:T(8,128)(2,1)S(1)} %bitcast.62), channel_id=1, source_target_pairs={{0,4},{4,8},{8,12},{12,16},{16,20},{20,24},{24,28},{1,5},{5,9},{9,... | collective-permute-start | bytes 49160 | tf_op jit(solution)/shard_map/ppermute | solution.py:18
  34.0 8.7 %all-to-all-start.1 = ((bf16[4,256,32]{1,2,0:T(8,128)(2,1)}), bf16[4,256,32]{1,2,0:T(8,128)(2,1)S(1)}, u32[]{:S(2)}, u32[]{:S(2)}) async-start(bf16[4,256,32]{1,2,0:T(8,128)(2,1)} %bitcast.48), calls=%async_computation.1 | async-start | bytes 131072 | tf_op jit(solution)/shard_map/all_to_all | solution.py:48
  38.4 13.1 %collective-permute-start.2 = (bf16[18,1,16,32]{3,2,1,0:T(8,128)(2,1)}, bf16[18,1,16,32]{3,2,1,0:T(8,128)(2,1)}, u32[]{:S(2)}, u32[]{:S(2)}) collective-permute-start(bf16[18,1,16,32]{3,2,1,0:T(8,128)(2,1)} %get-tuple-element.7), channel_id=1, source_target_pairs={{0,1},{1,2},{2,3},{4,5},{5,6},{6,7},{8,9},{9,10},{10,11},{12,13},{... | collective-permute-start | bytes 55304 | tf_op jit(solution)/shard_map/ppermute | solution.py:18
  41.4 10.1 %collective-permute-start.3 = (bf16[18,1,16,32]{3,2,1,0:T(8,128)(2,1)}, bf16[18,1,16,32]{3,2,1,0:T(8,128)(2,1)}, u32[]{:S(2)}, u32[]{:S(2)}) collective-permute-start(bf16[18,1,16,32]{3,2,1,0:T(8,128)(2,1)} %get-tuple-element.8), channel_id=1, source_target_pairs={{1,0},{2,1},{3,2},{5,4},{6,5},{7,6},{9,8},{10,9},{11,10},{13,12},{... | collective-permute-start | bytes 55304 | tf_op jit(solution)/shard_map/ppermute | solution.py:19
  51.5 2.7 %copy-start.1 = (f32[4097,32]{1,0:T(8,128)}, f32[4097,32]{1,0:T(8,128)S(1)}, u32[]{:S(2)}) copy-start(f32[4097,32]{1,0:T(8,128)S(1)} %scatter_custom_fusion) | copy-start | bytes 1573252
  61.3 0.7 copy-start.3
  66.6 1.6 %slice-start = ((f32[4097,32]{1,0:T(8,128)}), f32[4096,32]{1,0:T(8,128)S(1)}, s32[]{:S(2)}) async-start(f32[4097,32]{1,0:T(8,128)} %copy-done.1), calls=%async_computation.4 | async-start | bytes 4194304 | tf_op jit(solution)/shard_map/slice | solution.py:59
  69.3 6.7 %collective-permute-start.4 = (bf16[1,16,16,32]{3,1,2,0:T(8,128)(2,1)S(1)}, bf16[1,16,16,32]{3,1,2,0:T(8,128)(2,1)S(1)}, u32[]{:S(2)}, u32[]{:S(2)}) collective-permute-start(bf16[1,16,16,32]{3,1,2,0:T(8,128)(2,1)S(1)} %get-tuple-element.11), channel_id=1, source_target_pairs={{0,4},{4,8},{8,12},{12,16},{16,20},{20,24},{24,28},{1,5},{5,9},{9,... | collective-permute-start | bytes 49160 | tf_op jit(solution)/shard_map/ppermute | solution.py:18
  73.8 6.8 %collective-permute-start.5 = (bf16[1,16,16,32]{3,1,2,0:T(8,128)(2,1)S(1)}, bf16[1,16,16,32]{3,1,2,0:T(8,128)(2,1)S(1)}, u32[]{:S(2)}, u32[]{:S(2)}) collective-permute-start(bf16[1,16,16,32]{3,1,2,0:T(8,128)(2,1)S(1)} %get-tuple-element.12), channel_id=1, source_target_pairs={{4,0},{8,4},{12,8},{16,12},{20,16},{24,20},{28,24},{5,1},{9,5},{13... | collective-permute-start | bytes 49160 | tf_op jit(solution)/shard_map/ppermute | solution.py:19
  80.9 9.7 %collective-permute-start.6 = (bf16[18,1,16,32]{3,1,2,0:T(2,128)(2,1)S(1)}, bf16[18,1,16,32]{3,1,2,0:T(2,128)(2,1)S(1)}, u32[]{:S(2)}, u32[]{:S(2)}) collective-permute-start(bf16[18,1,16,32]{3,1,2,0:T(2,128)(2,1)S(1)} %get-tuple-element.5), channel_id=1, source_target_pairs={{0,1},{1,2},{2,3},{4,5},{5,6},{6,7},{8,9},{9,10},{10,11},{12,13},{... | collective-permute-start | bytes 55304 | tf_op jit(solution)/shard_map/ppermute | solution.py:18
  83.0 7.7 %collective-permute-start.7 = (bf16[18,1,16,32]{3,1,2,0:T(2,128)(2,1)S(1)}, bf16[18,1,16,32]{3,1,2,0:T(2,128)(2,1)S(1)}, u32[]{:S(2)}, u32[]{:S(2)}) collective-permute-start(bf16[18,1,16,32]{3,1,2,0:T(2,128)(2,1)S(1)} %get-tuple-element.6), channel_id=1, source_target_pairs={{1,0},{2,1},{3,2},{5,4},{6,5},{7,6},{9,8},{10,9},{11,10},{13,12},{... | collective-permute-start | bytes 55304 | tf_op jit(solution)/shard_map/ppermute | solution.py:19
where the time goes:
time: 115 us; the launch traced here: 114 us
  starting transfers between devices  30.7 us (27%)
  other arithmetic  30.5 us (27%)
  local copies, waits for them, and re-layouts  25.2 us (22%)
  blocking collectives  10.1 us (9%)
  matrix products  9.29 us (8%)
  waiting for transfers between devices  7.87 us (7%)
    ppermute x4, starting transfers between devices, extended(): before = lax.ppermute(last, axis, up)  14 us
    all_to_all x1, blocking collectives, per_device(): lax.all_to_all(grads, 'group', split_axis=0, concat_axis=0, tiled=True)  10.1 us
    conv_general_dilated x2, matrix products, convolve(): lax.conv_general_dilated(padded[None], weights, (1, 1, 1), 'VALID', dimen...  9.29 us
    gather x3, local copies, waits for them, and re-layouts, per_device(): grads = (table[index] / divisor[index][:, None]).astype(jnp.bfloat16)  9.13 us
    conv_general_dilated x9, local copies, waits for them, and re-layouts, convolve(): lax.conv_general_dilated(padded[None], weights, (1, 1, 1), 'VALID', dimen...  8.32 us
    scatter-add x1, other arithmetic, per_device(): jax.ops.segment_sum(cot_in.astype(jnp.float32), index, voxels + 1)[:voxels]  7.8 us
    scatter-add x1, other arithmetic, per_device(): sums = jax.ops.segment_sum(feats_in.astype(jnp.float32), index, voxels + 1)  7.22 us
    scatter-add x1, other arithmetic, per_device(): jax.ops.segment_sum(jnp.ones(index.shape, jnp.float32), index, voxels + 1)  6.76 us
  transfers between devices with their start and end apart: 11, of which 3 were waited for; matrix products, arithmetic and copies ran while one was open for 22% of the time, Pallas kernels for 0%

commit v1 on v0

v1 whole, which is shorter than its diff:
```python
import functools

import jax
import jax.numpy as jnp
from jax import lax
from jax.experimental import pallas as pl
from jax.experimental.pallas import tpu as pltpu
from jax.sharding import PartitionSpec as P

MESH = pl.DeviceIdType.MESH
F32 = jnp.float32
BF16 = jnp.bfloat16
SIDE = 16
C = 32
COLS = SIDE * SIDE
LANES = SIDE * C
HALF = LANES // 2
CAP = 256

WAYS = ((-1, 0), (1, 0), (0, -1), (0, 1), (-1, -1), (-1, 1), (1, -1), (1, 1))


def nt(a, b):
    return lax.dot_general(a, b, (((1,), (1,)), ((), ())), preferred_element_type=F32)


def nn(a, b):
    return jnp.dot(a, b, preferred_element_type=F32)


def kernel(
    n, ns, feats, cots, vox, weights, out,
    gotf, gotc, gotv, hot, masked, tiled, bmf, bef, bmb, beb,
    inner, hx, hy, xm, xe, xh, acc, gy, div, back,
    fs, fr, cs, cr, vs, vr, hs, hr, rs, rr,
):
    s = lax.axis_index("space")
    g = lax.axis_index("group")

    def exists(way):
        ok = None
        for d, at, size in ((way[0], s, ns), (way[1], g, n)):
            if d == 0:
                continue
            here = at > 0 if d < 0 else at < size - 1
            ok = here if ok is None else jnp.logical_and(ok, here)
        return ok

    def peer(d):
        return lax.rem(g + d, n)

    barrier = pltpu.get_barrier_semaphore()
    outer = [w for w in WAYS if w[0] != 0]
    for d in range(1, n):
        pl.semaphore_signal(barrier, inc=1, device_id=(s, peer(d)), device_id_type=MESH)
    for w in outer:
        @pl.when(exists(w))
        def _(w=w):
            pl.semaphore_signal(barrier, inc=1, device_id=(s + w[0], g + w[1]), device_id_type=MESH)

    peers = n - 1
    for w in outer:
        peers = peers + jnp.where(exists(w), 1, 0)
    pl.semaphore_wait(barrier, peers)

    def slots_of(k):
        return pl.ds(pl.multiple_of(k * CAP, CAP), CAP)

    def copy_v(d):
        return pltpu.make_async_remote_copy(
            src_ref=vox.at[peer(d)], dst_ref=gotv.at[d], send_sem=vs.at[d], recv_sem=vr.at[d],
            device_id=(s, peer(d)), device_id_type=MESH)

    def copy_f(d):
        return pltpu.make_async_remote_copy(
            src_ref=feats.at[:, slots_of(peer(d))], dst_ref=gotf.at[d], send_sem=fs.at[d], recv_sem=fr.at[d],
            device_id=(s, peer(d)), device_id_type=MESH)

    def copy_c(d):
        return pltpu.make_async_remote_copy(
            src_ref=cots.at[:, slots_of(peer(d))], dst_ref=gotc.at[d], send_sem=cs.at[d], recv_sem=cr.at[d],
            device_id=(s, peer(d)), device_id_type=MESH)

    for d in range(1, n):
        copy_v(d).start()
        copy_f(d).start()
        copy_c(d).start()

    spread = jnp.where(
        (lax.broadcasted_iota(jnp.int32, (C, HALF), 1) & (C - 1)) == lax.broadcasted_iota(jnp.int32, (C, HALF), 0),
        1.0, 0.0).astype(BF16)
    tiled[...] = nn(weights[...], spread)
    block = lax.broadcasted_iota(jnp.int32, (C, HALF), 1) // C
    narrow = lax.broadcasted_iota(jnp.int32, (C, 128), 1) // C
    none = jnp.zeros((C, 128), BF16)
    wide = HALF // C

    def tile(dx, dy, dz):
        a = (dx * 3 + dy) * 3 + dz
        return tiled[a * C : (a + 1) * C, :]

    for dy in range(3):
        for dz in range(3):
            w0, w1, w2 = (tile(dx, dy, dz) for dx in range(3))
            fy, fz = 2 - dy, 2 - dz
            for i in range(wide):
                band = jnp.where(
                    block == i, w1, jnp.where(block == i - 1, w2, jnp.where(block == i + 1, w0, 0.0))
                ).astype(BF16)
                bmf[dy, dz * HALF + i * C : dz * HALF + (i + 1) * C, :] = band
                bmb[fy, i * C : (i + 1) * C, fz * HALF : (fz + 1) * HALF] = band
                if i == wide - 1:
                    edge = jnp.where(narrow == 0, w0[:, :128], 0.0).astype(BF16)
                elif i == 0:
                    edge = jnp.where(narrow == 3, w2[:, :128], 0.0).astype(BF16)
                else:
                    edge = none
                beb[fy, i * C : (i + 1) * C, fz * 128 : (fz + 1) * 128] = edge
            bef[dy, dz * 128 : dz * 128 + C, :] = jnp.where(block == wide - 1, w2, 0.0).astype(BF16)
            bef[dy, dz * 128 + C : dz * 128 + 3 * C, :] = jnp.zeros((2 * C, HALF), BF16)
            bef[dy, dz * 128 + 3 * C : dz * 128 + 4 * C, :] = jnp.where(block == 0, w0, 0.0).astype(BF16)

    for p in range(2):
        for side, d in ((0, -1), (1, 1)):
            @pl.when(jnp.logical_not(exists((d, 0))))
            def _(p=p, side=side):
                hx[p, side] = jnp.zeros((COLS + 2 * SIDE, 128), BF16)

            @pl.when(jnp.logical_not(exists((0, d))))
            def _(p=p, side=side):
                hy[p, side] = jnp.zeros((SIDE, LANES), BF16)
                r0 = side * (COLS + SIDE)
                for q in range(2):
                    hx[p, q, r0 : r0 + SIDE, :] = jnp.zeros((SIDE, 128), BF16)
    for b in range(2):
        xm[b, 0:SIDE, :] = jnp.zeros((SIDE, 3 * HALF), BF16)
        xm[b, COLS + SIDE : COLS + 2 * SIDE, :] = jnp.zeros((SIDE, 3 * HALF), BF16)

    row = lax.broadcasted_iota(jnp.int32, (COLS, CAP), 0)

    def place(d, v, f, c):
        lo = v & (COLS - 1)
        hi = v >> 8
        at = slice(d * CAP, (d + 1) * CAP)
        hot[:, at] = jnp.where(row == lo, 1.0, 0.0).astype(BF16)
        f = f.astype(F32)
        c = c.astype(F32)
        hi = jnp.broadcast_to(hi, (C, CAP))
        for x in range(SIDE):
            hit = hi == x
            for q, val in enumerate((f, c, 1.0)):
                r0 = q * LANES + x * C
                masked[r0 : r0 + C, at] = jnp.where(hit, val, 0.0).astype(BF16)

    place(0, vox[g], feats[:, slots_of(g)], cots[:, slots_of(g)])
    for d in range(1, n):
        copy_v(d).wait_recv()
        copy_f(d).wait_recv()
        copy_c(d).wait_recv()
        place(d, gotv[d], gotf[d], gotc[d])

    pooled = nt(hot[...], masked[...])
    count = jnp.maximum(pooled[:, 2 * LANES :], 1.0)
    div[...] = count
    gy[...] = pooled[:, LANES : 2 * LANES]
    mean = (pooled[:, :LANES] / count).astype(BF16)

    def shifts(val):
        z = lax.broadcasted_iota(jnp.int32, val.shape, 0) & (SIDE - 1)
        down = jnp.where(z == 0, 0.0, pltpu.roll(val, 1, 0))
        up = jnp.where(z == SIDE - 1, 0.0, pltpu.roll(val, val.shape[0] - 1, 0))
        return down.astype(BF16), val.astype(BF16), up.astype(BF16)

    def halo(p, k):
        dx, dy = WAYS[k]
        src_rows = pl.ds(0, SIDE) if dy < 0 else pl.ds(COLS - SIDE, SIDE) if dy > 0 else pl.ds(0, COLS)
        if dx == 0:
            src = inner.at[p, src_rows, :]
            dst = hy.at[p, 0 if dy > 0 else 1]
        else:
            src = inner.at[p, src_rows, pl.ds(0 if dx < 0 else LANES - 128, 128)]
            dst_rows = pl.ds(0, SIDE) if dy > 0 else pl.ds(COLS + SIDE, SIDE) if dy < 0 else pl.ds(SIDE, COLS)
            dst = hx.at[p, 0 if dx > 0 else 1, dst_rows, :]
        return pltpu.make_async_remote_copy(
            src_ref=src, dst_ref=dst, send_sem=hs.at[p, k], recv_sem=hr.at[p, k],
            device_id=(s + dx, g + dy), device_id_type=MESH)

    def convolve(p, val, main, edges, dot):
        inner[p] = val
        for k, w in enumerate(WAYS):
            @pl.when(exists(w))
            def _(k=k):
                halo(p, k).start()
        for b in range(2):
            for j, part in enumerate(shifts(val[:, b * HALF : (b + 1) * HALF].astype(F32))):
                xm[b, SIDE : SIDE + COLS, j * HALF : (j + 1) * HALF] = part
        total = None
        for dy in range(3):
            lhs = xm[:, dy * SIDE : dy * SIDE + COLS, :].reshape(2 * COLS, 3 * HALF)
            term = dot(lhs, main[dy])
            total = term if total is None else total + term
        acc[...] = total.reshape(2, COLS, HALF)
        for k, w in enumerate(WAYS):
            @pl.when(exists((-w[0], -w[1])))
            def _(k=k):
                halo(p, k).wait_recv()
        for side in range(2):
            rim = hy[p, side].astype(F32)
            for b in range(2):
                for j, part in enumerate(shifts(rim[:, b * HALF : (b + 1) * HALF])):
                    xh[side, b, :, j * HALF : (j + 1) * HALF] = part
        span = COLS + 2 * SIDE
        first = lax.broadcasted_iota(jnp.int32, (span, 128), 1) < C
        for b in range(2):
            at = slice(HALF, HALF + 128) if b == 0 else slice(HALF - 128, HALF)
            own = jnp.concatenate([hy[p, 0, :, at], inner[p, :, at], hy[p, 1, :, at]], axis=0).astype(F32)
            far = hx[p, b].astype(F32)
            edge = jnp.where(first, own, far) if b == 0 else jnp.where(first, far, own)
            for j, part in enumerate(shifts(edge)):
                xe[b, :, j * 128 : (j + 1) * 128] = part
        total = None
        for dy in range(3):
            lhs = xe[:, dy * SIDE : dy * SIDE + COLS, :].reshape(2 * COLS, 3 * 128)
            term = dot(lhs, edges[dy])
            total = term if total is None else total + term
        acc[...] += total.reshape(2, COLS, HALF)
        for side, dy, r0 in ((0, 0, 0), (1, 2, COLS - SIDE)):
            term = dot(xh[side].reshape(2 * SIDE, 3 * HALF), main[dy])
            acc[:, r0 : r0 + SIDE, :] += term.reshape(2, SIDE, HALF)

    convolve(0, mean, bmf, bef, nn)
    parts = []
    for b in range(2):
        o = acc[b]
        sig = 1.0 / (1.0 + jnp.exp(-o))
        parts.append((gy[:, b * HALF : (b + 1) * HALF] * sig * (1.0 + o * (1.0 - sig))).astype(BF16))
    convolve(1, jnp.concatenate(parts, axis=1), bmb, beb, nt)

    grad = jnp.concatenate([acc[b] / div[:, b * HALF : (b + 1) * HALF] for b in range(2)], axis=1)
    grad = jnp.transpose(grad).astype(BF16)

    def copy_r(d):
        return pltpu.make_async_remote_copy(
            src_ref=back.at[d], dst_ref=out.at[:, slots_of(g)], send_sem=rs.at[d], recv_sem=rr.at[d],
            device_id=(s, peer(n - d)), device_id_type=MESH)

    for d in list(range(1, n)) + [0]:
        v = vox[g] if d == 0 else gotv[d]
        hi = jnp.broadcast_to(v >> 8, (C, CAP))
        rows = nn(grad, hot[:, d * CAP : (d + 1) * CAP])
        picked = jnp.zeros((C, CAP), F32)
        for x in range(SIDE):
            picked = picked + jnp.where(hi == x, rows[x * C : (x + 1) * C], 0.0)
        if d == 0:
            out[:, slots_of(g)] = picked.astype(BF16)
        else:
            back[d] = picked.astype(BF16)
            copy_r(d).start()
    for d in range(1, n):
        copy_r(d).wait_recv()
    for d in range(1, n):
        copy_v(d).wait_send()
        copy_f(d).wait_send()
        copy_c(d).wait_send()
        copy_r(d).wait_send()
    for p in range(2):
        for k, w in enumerate(WAYS):
            @pl.when(exists(w))
            def _(p=p, k=k):
                halo(p, k).wait_send()


def per_device(n, ns, point_feats, point_voxel, cotangent, weights):
    slots = n * CAP
    span = COLS + 2 * SIDE
    vm = pltpu.VMEM
    dma = pltpu.SemaphoreType.DMA
    return pl.pallas_call(
        functools.partial(kernel, n, ns),
        out_shape=jax.ShapeDtypeStruct((C, slots), BF16),
        in_specs=[pl.BlockSpec(memory_space=vm)] * 4,
        out_specs=pl.BlockSpec(memory_space=vm),
        scratch_shapes=[
            vm((n, C, CAP), BF16),
            vm((n, C, CAP), BF16),
            vm((n, 1, CAP), jnp.int32),
            vm((COLS, slots), BF16),
            vm((3 * LANES, slots), BF16),
            vm((27 * C, HALF), F32),
            vm((3, 3 * HALF, HALF), BF16),
            vm((3, 3 * 128, HALF), BF16),
            vm((3, HALF, 3 * HALF), BF16),
            vm((3, HALF, 3 * 128), BF16),
            vm((2, COLS, LANES), BF16),
            vm((2, 2, span, 128), BF16),
            vm((2, 2, SIDE, LANES), BF16),
            vm((2, span, 3 * HALF), BF16),
            vm((2, span, 3 * 128), BF16),
            vm((2, 2, SIDE, 3 * HALF), BF16),
            vm((2, COLS, HALF), F32),
            vm((COLS, LANES), F32),
            vm((COLS, LANES), F32),
            vm((n, C, CAP), BF16),
            dma((n,)), dma((n,)), dma((n,)), dma((n,)), dma((n,)), dma((n,)),
            dma((2, 8)), dma((2, 8)), dma((n,)), dma((n,)),
        ],
        compiler_params=pltpu.CompilerParams(
            collective_id=0, has_side_effects=True, vmem_limit_bytes=48 * 2**20
        ),
    )(point_feats.T, cotangent.T, point_voxel.reshape(n, 1, CAP), weights.reshape(27 * C, C)).T


def solution(mesh):
    n, ns = mesh.shape["group"], mesh.shape["space"]
    placed = (P(("space", "group"), None), P(("space", "group")), P(("space", "group"), None), P())
    return jax.shard_map(
        functools.partial(per_device, n, ns),
        mesh=mesh,
        in_specs=placed,
        out_specs=P(("space", "group"), None),
        check_vma=False,
    )
```

time: 115 us -> 27.5 us (0.24)
  starting transfers between devices: 30.7 us -> 0 us
  other arithmetic: 30.5 us -> 0 us
  Pallas kernels: 0 us -> 23.1 us
  local copies, waits for them, and re-layouts: 25.2 us -> 3.93 us
  blocking collectives: 10.1 us -> 0 us
  matrix products: 9.29 us -> 0 us
  waiting for transfers between devices: 7.87 us -> 0 us
    pallas_call x0 -> x1, Pallas kernels: none -> 23.1 us  [per_device(): pl.pallas_call(functools.partial(kernel, n, ns), out_shape=jax.ShapeDtype...]
    scatter-add x3 -> x0, other arithmetic: 21.8 us -> none  [the longest x1 7.8 us: per_device(): jax.ops.segment_sum(cot_in.astype(jnp.float32), index, voxels + 1)[:voxels]]
    ppermute x8 -> x0, starting transfers between devices: 19.4 us -> none  [the longest x4 14 us: extended(): before = lax.ppermute(last, axis, up)]
    all_to_all x3 -> x0, starting transfers between devices: 11.3 us -> none  [the longest x1 4.37 us: per_device(): lax.all_to_all(point_voxel, 'group', split_axis=0, concat_axis=0, tiled=T...]
    all_to_all x1 -> x0, blocking collectives: 10.1 us -> none  [per_device(): lax.all_to_all(grads, 'group', split_axis=0, concat_axis=0, tiled=True)]
    conv_general_dilated x2 -> x0, matrix products: 9.29 us -> none  [convolve(): lax.conv_general_dilated(padded[None], weights, (1, 1, 1), 'VALID', dimen...]
    gather x3 -> x0, local copies, waits for them, and re-layouts: 9.13 us -> none  [per_device(): grads = (table[index] / divisor[index][:, None]).astype(jnp.bfloat16)]
    conv_general_dilated x9 -> x0, local copies, waits for them, and re-layouts: 8.32 us -> none  [convolve(): lax.conv_general_dilated(padded[None], weights, (1, 1, 1), 'VALID', dimen...]
  transfers between devices with their start and end apart: 11 -> 0, of which waited for: 3 -> 0; matrix products, arithmetic and copies ran while one was open for 22% -> 0% of each run, Pallas kernels for 0% -> 0%
where the time goes in v1:
time: 27.5 us; the launch traced here: 27 us
  Pallas kernels  23.1 us (84%)
  local copies, waits for them, and re-layouts  3.93 us (14%)
    pallas_call x1, Pallas kernels, per_device(): pl.pallas_call(functools.partial(kernel, n, ns), out_shape=jax.ShapeDtype...  23.1 us
    unnamed x9, local copies, waits for them, and re-layouts  3.93 us

profile of v1, /device:TPU:0, one launch (start us, length us, event | category | flops | bytes accessed | tf_op | source)
XLA Modules:
  0.0 27.0 jit_solution(11042261443776515807)
XLA Ops:
  0.0 0.0 copy-start.3
  0.0 0.7 %copy-done.3 = s32[1024]{0:T(1024)S(1)} copy-done((s32[1024]{0:T(1024)S(1)}, s32[1024]{0:T(1024)}, u32[]{:S(2)}) %copy-start.3) | copy-done | bytes 4120
  0.7 0.0 copy-start
  0.7 0.9 %copy-done = bf16[3,3,3,32,32]{4,3,2,1,0:T(8,128)(2,1)S(1)} copy-done((bf16[3,3,3,32,32]{4,3,2,1,0:T(8,128)(2,1)S(1)}, bf16[3,3,3,32,32]{4,3,2,1,0:T(8,128)(2,1)}, u32[]{:S(2)}) %copy-start) | copy-done | bytes 55320
  1.6 0.0 copy-start.1
  1.6 0.8 %copy-done.1 = bf16[1024,32]{0,1:T(8,128)(2,1)S(1)} copy-done((bf16[1024,32]{0,1:T(8,128)(2,1)S(1)}, bf16[1024,32]{0,1:T(8,128)(2,1)}, u32[]{:S(2)}) %copy-start.1) | copy-done | bytes 65560
  2.5 0.0 copy-start.2
  2.5 0.8 %copy-done.2 = bf16[1024,32]{0,1:T(8,128)(2,1)S(1)} copy-done((bf16[1024,32]{0,1:T(8,128)(2,1)S(1)}, bf16[1024,32]{0,1:T(8,128)(2,1)}, u32[]{:S(2)}) %copy-start.2) | copy-done | bytes 65560
  3.3 23.1 %shard_map.46 = bf16[32,1024]{1,0:T(8,128)(2,1)S(1)} custom-call(bf16[32,1024]{1,0:T(8,128)(2,1)S(1)} %bitcast.7, bf16[32,1024]{1,0:T(8,128)(2,1)S(1)} %bitcast.8, s32[4,1,256]{2,1,0:T(1,128)S(1)} %bitcast.9, bf16[864,32]{1,0:T(8,128)(2,1)S(1)} %bitcast.6), custom_call_target="tpu_custom_call" | custom-call | tf_op jit(solution)/shard_map/pallas_call | solution.py:278
  26.4 0.6 %copy.6 = bf16[1024,32]{0,1:T(8,128)(2,1)} copy(bf16[1024,32]{0,1:T(8,128)(2,1)S(1)} %bitcast.5) | data formatting | bytes 131072
Async XLA Ops:
  0.0 0.7 %copy-start.3 = (s32[1024]{0:T(1024)S(1)}, s32[1024]{0:T(1024)}, u32[]{:S(2)}) copy-start(s32[1024]{0:T(1024)} %param.5) | copy-start | bytes 12292
  0.7 0.9 %copy-start = (bf16[3,3,3,32,32]{4,3,2,1,0:T(8,128)(2,1)S(1)}, bf16[3,3,3,32,32]{4,3,2,1,0:T(8,128)(2,1)}, u32[]{:S(2)}) copy-start(bf16[3,3,3,32,32]{4,3,2,1,0:T(8,128)(2,1)} %param.7) | copy-start | bytes 165892
  1.6 0.8 %copy-start.1 = (bf16[1024,32]{0,1:T(8,128)(2,1)S(1)}, bf16[1024,32]{0,1:T(8,128)(2,1)}, u32[]{:S(2)}) copy-start(bf16[1024,32]{0,1:T(8,128)(2,1)} %param.4) | copy-start | bytes 196612
  2.5 0.8 %copy-start.2 = (bf16[1024,32]{0,1:T(8,128)(2,1)S(1)}, bf16[1024,32]{0,1:T(8,128)(2,1)}, u32[]{:S(2)}) copy-start(bf16[1024,32]{0,1:T(8,128)(2,1)} %param.6) | copy-start | bytes 196612

commit v2 on v1

--- a/solution.py
+++ b/solution.py
@@ -30,9 +30,9 @@
 
 def kernel(
     n, ns, feats, cots, vox, weights, out,
-    gotf, gotc, gotv, hot, masked, tiled, bmf, bef, bmb, beb,
-    inner, hx, hy, xm, xe, xh, acc, gy, div, back,
-    fs, fr, cs, cr, vs, vr, hs, hr, rs, rr,
+    gotf, gotc, gotv, w_in, hot, masked, sums, tiled, bmf, bef, bmb, beb,
+    inner, packed, hx, hc, hy, xm, xe, xh, acc, gy, div, back,
+    local, fs, fr, cs, cr, vs, vr, hs, hr, rs, rr,
 ):
     s = lax.axis_index("space")
     g = lax.axis_index("group")
@@ -49,6 +49,18 @@
     def peer(d):
         return lax.rem(g + d, n)
 
+    def slots_of(k):
+        return pl.ds(pl.multiple_of(k * CAP, CAP), CAP)
+
+    own_copies = [
+        pltpu.make_async_copy(src, dst, local.at[i])
+        for i, (src, dst) in enumerate((
+            (weights, w_in), (vox.at[g], gotv.at[0]),
+            (feats.at[:, slots_of(g)], gotf.at[0]), (cots.at[:, slots_of(g)], gotc.at[0])))
+    ]
+    for c in own_copies:
+        c.start()
+
     barrier = pltpu.get_barrier_semaphore()
     outer = [w for w in WAYS if w[0] != 0]
     for d in range(1, n):
@@ -63,9 +75,6 @@
         peers = peers + jnp.where(exists(w), 1, 0)
     pl.semaphore_wait(barrier, peers)
 
-    def slots_of(k):
-        return pl.ds(pl.multiple_of(k * CAP, CAP), CAP)
-
     def copy_v(d):
         return pltpu.make_async_remote_copy(
             src_ref=vox.at[peer(d)], dst_ref=gotv.at[d], send_sem=vs.at[d], recv_sem=vr.at[d],
@@ -84,12 +93,15 @@
     for d in range(1, n):
         copy_v(d).start()
         copy_f(d).start()
+    for d in range(1, n):
         copy_c(d).start()
+    for c in own_copies:
+        c.wait()
 
     spread = jnp.where(
         (lax.broadcasted_iota(jnp.int32, (C, HALF), 1) & (C - 1)) == lax.broadcasted_iota(jnp.int32, (C, HALF), 0),
         1.0, 0.0).astype(BF16)
-    tiled[...] = nn(weights[...], spread)
+    tiled[...] = nn(w_in[...], spread)
     block = lax.broadcasted_iota(jnp.int32, (C, HALF), 1) // C
     narrow = lax.broadcasted_iota(jnp.int32, (C, 128), 1) // C
     none = jnp.zeros((C, 128), BF16)
@@ -99,71 +111,90 @@
         a = (dx * 3 + dy) * 3 + dz
         return tiled[a * C : (a + 1) * C, :]
 
-    for dy in range(3):
-        for dz in range(3):
-            w0, w1, w2 = (tile(dx, dy, dz) for dx in range(3))
-            fy, fz = 2 - dy, 2 - dz
-            for i in range(wide):
-                band = jnp.where(
-                    block == i, w1, jnp.where(block == i - 1, w2, jnp.where(block == i + 1, w0, 0.0))
-                ).astype(BF16)
-                bmf[dy, dz * HALF + i * C : dz * HALF + (i + 1) * C, :] = band
-                bmb[fy, i * C : (i + 1) * C, fz * HALF : (fz + 1) * HALF] = band
-                if i == wide - 1:
-                    edge = jnp.where(narrow == 0, w0[:, :128], 0.0).astype(BF16)
-                elif i == 0:
-                    edge = jnp.where(narrow == 3, w2[:, :128], 0.0).astype(BF16)
-                else:
-                    edge = none
-                beb[fy, i * C : (i + 1) * C, fz * 128 : (fz + 1) * 128] = edge
-            bef[dy, dz * 128 : dz * 128 + C, :] = jnp.where(block == wide - 1, w2, 0.0).astype(BF16)
-            bef[dy, dz * 128 + C : dz * 128 + 3 * C, :] = jnp.zeros((2 * C, HALF), BF16)
-            bef[dy, dz * 128 + 3 * C : dz * 128 + 4 * C, :] = jnp.where(block == 0, w0, 0.0).astype(BF16)
+    def band(i, w0, w1, w2):
+        inside = jnp.where(block == i, w1, jnp.where(block == i - 1, w2, jnp.where(block == i + 1, w0, 0.0)))
+        return inside.astype(BF16)
+
+    def forward_bands():
+        for dy in range(3):
+            for dz in range(3):
+                w0, w1, w2 = (tile(dx, dy, dz) for dx in range(3))
+                for i in range(wide):
+                    bmf[dy, dz * HALF + i * C : dz * HALF + (i + 1) * C, :] = band(i, w0, w1, w2)
+                bef[dy, dz * 128 : dz * 128 + C, :] = jnp.where(block == wide - 1, w2, 0.0).astype(BF16)
+                bef[dy, dz * 128 + C : dz * 128 + 3 * C, :] = jnp.zeros((2 * C, HALF), BF16)
+                bef[dy, dz * 128 + 3 * C : dz * 128 + 4 * C, :] = jnp.where(block == 0, w0, 0.0).astype(BF16)
+
+    def backward_bands():
+        for fy in range(3):
+            for fz in range(3):
+                w0, w1, w2 = (tile(dx, 2 - fy, 2 - fz) for dx in range(3))
+                for i in range(wide):
+                    at = slice(i * C, (i + 1) * C)
+                    bmb[fy, at, fz * HALF : (fz + 1) * HALF] = band(i, w0, w1, w2)
+                    if i == wide - 1:
+                        edge = jnp.where(narrow == 0, w0[:, :128], 0.0).astype(BF16)
+                    elif i == 0:
+                        edge = jnp.where(narrow == 3, w2[:, :128], 0.0).astype(BF16)
+                    else:
+                        edge = none
+                    beb[fy, at, fz * 128 : (fz + 1) * 128] = edge
+
+    forward_bands()
 
     for p in range(2):
         for side, d in ((0, -1), (1, 1)):
             @pl.when(jnp.logical_not(exists((d, 0))))
             def _(p=p, side=side):
-                hx[p, side] = jnp.zeros((COLS + 2 * SIDE, 128), BF16)
+                hx[p, side] = jnp.zeros((COLS // 4, 128), BF16)
 
             @pl.when(jnp.logical_not(exists((0, d))))
             def _(p=p, side=side):
                 hy[p, side] = jnp.zeros((SIDE, LANES), BF16)
-                r0 = side * (COLS + SIDE)
-                for q in range(2):
-                    hx[p, q, r0 : r0 + SIDE, :] = jnp.zeros((SIDE, 128), BF16)
+
+            for side2, d2 in ((0, -1), (1, 1)):
+                @pl.when(jnp.logical_not(exists((d, d2))))
+                def _(p=p, side=side, side2=side2):
+                    hc[p, side, side2] = jnp.zeros((SIDE, 128), BF16)
     for b in range(2):
         xm[b, 0:SIDE, :] = jnp.zeros((SIDE, 3 * HALF), BF16)
         xm[b, COLS + SIDE : COLS + 2 * SIDE, :] = jnp.zeros((SIDE, 3 * HALF), BF16)
 
     row = lax.broadcasted_iota(jnp.int32, (COLS, CAP), 0)
 
-    def place(d, v, f, c):
-        lo = v & (COLS - 1)
-        hi = v >> 8
-        at = slice(d * CAP, (d + 1) * CAP)
-        hot[:, at] = jnp.where(row == lo, 1.0, 0.0).astype(BF16)
-        f = f.astype(F32)
-        c = c.astype(F32)
-        hi = jnp.broadcast_to(hi, (C, CAP))
+    def mask(d, q, val):
+        hi = jnp.broadcast_to(gotv[d] >> 8, (C, CAP))
         for x in range(SIDE):
-            hit = hi == x
-            for q, val in enumerate((f, c, 1.0)):
-                r0 = q * LANES + x * C
-                masked[r0 : r0 + C, at] = jnp.where(hit, val, 0.0).astype(BF16)
-
-    place(0, vox[g], feats[:, slots_of(g)], cots[:, slots_of(g)])
+            r0 = q * LANES + x * C
+            masked[d, r0 : r0 + C, :] = jnp.where(hi == x, val, 0.0).astype(BF16)
+
+    def pool_feats(d):
+        hot[d] = jnp.where(row == (gotv[d] & (COLS - 1)), 1.0, 0.0).astype(BF16)
+        mask(d, 0, gotf[d].astype(F32))
+        mask(d, 1, 1.0)
+        term = nt(hot[d], masked[d, 0 : 2 * LANES, :])
+        if d == 0:
+            sums[...] = term
+        else:
+            sums[...] += term
+
+    def pool_cots(d):
+        mask(d, 2, gotc[d].astype(F32))
+        term = nt(hot[d], masked[d, 2 * LANES :, :])
+        if d == 0:
+            gy[...] = term
+        else:
+            gy[...] += term
+
+    pool_feats(0)
     for d in range(1, n):
         copy_v(d).wait_recv()
         copy_f(d).wait_recv()
-        copy_c(d).wait_recv()
-        place(d, gotv[d], gotf[d], gotc[d])
-
-    pooled = nt(hot[...], masked[...])
-    count = jnp.maximum(pooled[:, 2 * LANES :], 1.0)
+        pool_feats(d)
+
+    count = jnp.maximum(sums[:, LANES:], 1.0)
     div[...] = count
-    gy[...] = pooled[:, LANES : 2 * LANES]
-    mean = (pooled[:, :LANES] / count).astype(BF16)
+    mean = (sums[:, :LANES] / count).astype(BF16)
 
     def shifts(val):
         z = lax.broadcasted_iota(jnp.int32, val.shape, 0) & (SIDE - 1)
@@ -171,22 +202,42 @@
         up = jnp.where(z == SIDE - 1, 0.0, pltpu.roll(val, val.shape[0] - 1, 0))
         return down.astype(BF16), val.astype(BF16), up.astype(BF16)
 
+    lane = lax.broadcasted_iota(jnp.int32, (COLS // 4, 128), 1) // C
+
+    def pack(val, at):
+        whole = None
+        for q in range(4):
+            part = val[q * (COLS // 4) : (q + 1) * (COLS // 4), :]
+            if q != at:
+                part = pltpu.roll(part, (q - at) % 4 * C, 1)
+            whole = part if whole is None else jnp.where(lane == q, part, whole)
+        return whole.astype(BF16)
+
+    def unpack(val, at):
+        val = val.astype(F32)
+        return jnp.concatenate(
+            [val if q == at else pltpu.roll(val, (at - q) % 4 * C, 1) for q in range(4)], axis=0)
+
     def halo(p, k):
         dx, dy = WAYS[k]
-        src_rows = pl.ds(0, SIDE) if dy < 0 else pl.ds(COLS - SIDE, SIDE) if dy > 0 else pl.ds(0, COLS)
+        src_rows = pl.ds(0, SIDE) if dy < 0 else pl.ds(COLS - SIDE, SIDE)
         if dx == 0:
             src = inner.at[p, src_rows, :]
             dst = hy.at[p, 0 if dy > 0 else 1]
+        elif dy == 0:
+            src = packed.at[p, 0 if dx < 0 else 1]
+            dst = hx.at[p, 0 if dx > 0 else 1]
         else:
             src = inner.at[p, src_rows, pl.ds(0 if dx < 0 else LANES - 128, 128)]
-            dst_rows = pl.ds(0, SIDE) if dy > 0 else pl.ds(COLS + SIDE, SIDE) if dy < 0 else pl.ds(SIDE, COLS)
-            dst = hx.at[p, 0 if dx > 0 else 1, dst_rows, :]
+            dst = hc.at[p, 0 if dx > 0 else 1, 0 if dy > 0 else 1]
         return pltpu.make_async_remote_copy(
             src_ref=src, dst_ref=dst, send_sem=hs.at[p, k], recv_sem=hr.at[p, k],
             device_id=(s + dx, g + dy), device_id_type=MESH)
 
-    def convolve(p, val, main, edges, dot):
+    def convolve(p, val, main, edges, dot, meanwhile):
         inner[p] = val
+        packed[p, 0] = pack(val[:, 0:128].astype(F32), 0)
+        packed[p, 1] = pack(val[:, LANES - 128 :].astype(F32), 3)
         for k, w in enumerate(WAYS):
             @pl.when(exists(w))
             def _(k=k):
@@ -200,6 +251,7 @@
             term = dot(lhs, main[dy])
             total = term if total is None else total + term
         acc[...] = total.reshape(2, COLS, HALF)
+        meanwhile()
         for k, w in enumerate(WAYS):
             @pl.when(exists((-w[0], -w[1])))
             def _(k=k):
@@ -214,7 +266,8 @@
         for b in range(2):
             at = slice(HALF, HALF + 128) if b == 0 else slice(HALF - 128, HALF)
             own = jnp.concatenate([hy[p, 0, :, at], inner[p, :, at], hy[p, 1, :, at]], axis=0).astype(F32)
-            far = hx[p, b].astype(F32)
+            far = jnp.concatenate(
+                [hc[p, b, 0].astype(F32), unpack(hx[p, b], 0 if b else 3), hc[p, b, 1].astype(F32)], axis=0)
             edge = jnp.where(first, own, far) if b == 0 else jnp.where(first, far, own)
             for j, part in enumerate(shifts(edge)):
                 xe[b, :, j * 128 : (j + 1) * 128] = part
@@ -228,13 +281,20 @@
             term = dot(xh[side].reshape(2 * SIDE, 3 * HALF), main[dy])
             acc[:, r0 : r0 + SIDE, :] += term.reshape(2, SIDE, HALF)
 
-    convolve(0, mean, bmf, bef, nn)
+    def first_wait():
+        for d in range(n):
+            if d:
+                copy_c(d).wait_recv()
+            pool_cots(d)
+        backward_bands()
+
+    convolve(0, mean, bmf, bef, nn, first_wait)
     parts = []
     for b in range(2):
         o = acc[b]
         sig = 1.0 / (1.0 + jnp.exp(-o))
         parts.append((gy[:, b * HALF : (b + 1) * HALF] * sig * (1.0 + o * (1.0 - sig))).astype(BF16))
-    convolve(1, jnp.concatenate(parts, axis=1), bmb, beb, nt)
+    convolve(1, jnp.concatenate(parts, axis=1), bmb, beb, nt, lambda: None)
 
     grad = jnp.concatenate([acc[b] / div[:, b * HALF : (b + 1) * HALF] for b in range(2)], axis=1)
     grad = jnp.transpose(grad).astype(BF16)
@@ -245,9 +305,8 @@
             device_id=(s, peer(n - d)), device_id_type=MESH)
 
     for d in list(range(1, n)) + [0]:
-        v = vox[g] if d == 0 else gotv[d]
-        hi = jnp.broadcast_to(v >> 8, (C, CAP))
-        rows = nn(grad, hot[:, d * CAP : (d + 1) * CAP])
+        hi = jnp.broadcast_to(gotv[d] >> 8, (C, CAP))
+        rows = nn(grad, hot[d])
         picked = jnp.zeros((C, CAP), F32)
         for x in range(SIDE):
             picked = picked + jnp.where(hi == x, rows[x * C : (x + 1) * C], 0.0)
@@ -278,21 +337,25 @@
     return pl.pallas_call(
         functools.partial(kernel, n, ns),
         out_shape=jax.ShapeDtypeStruct((C, slots), BF16),
-        in_specs=[pl.BlockSpec(memory_space=vm)] * 4,
+        in_specs=[pl.BlockSpec(memory_space=pltpu.HBM)] * 4,
         out_specs=pl.BlockSpec(memory_space=vm),
         scratch_shapes=[
             vm((n, C, CAP), BF16),
             vm((n, C, CAP), BF16),
             vm((n, 1, CAP), jnp.int32),
-            vm((COLS, slots), BF16),
-            vm((3 * LANES, slots), BF16),
+            vm((27 * C, C), BF16),
+            vm((n, COLS, CAP), BF16),
+            vm((n, 3 * LANES, CAP), BF16),
+            vm((COLS, 2 * LANES), F32),
             vm((27 * C, HALF), F32),
             vm((3, 3 * HALF, HALF), BF16),
             vm((3, 3 * 128, HALF), BF16),
             vm((3, HALF, 3 * HALF), BF16),
             vm((3, HALF, 3 * 128), BF16),
             vm((2, COLS, LANES), BF16),
-            vm((2, 2, span, 128), BF16),
+            vm((2, 2, COLS // 4, 128), BF16),
+            vm((2, 2, COLS // 4, 128), BF16),
+            vm((2, 2, 2, SIDE, 128), BF16),
             vm((2, 2, SIDE, LANES), BF16),
             vm((2, span, 3 * HALF), BF16),
             vm((2, span, 3 * 128), BF16),
@@ -301,7 +364,7 @@
             vm((COLS, LANES), F32),
             vm((COLS, LANES), F32),
             vm((n, C, CAP), BF16),
-            dma((n,)), dma((n,)), dma((n,)), dma((n,)), dma((n,)), dma((n,)),
+            dma((4,)), dma((n,)), dma((n,)), dma((n,)), dma((n,)), dma((n,)), dma((n,)),
             dma((2, 8)), dma((2, 8)), dma((n,)), dma((n,)),
         ],
         compiler_params=pltpu.CompilerParams(

time: 27.5 us -> 24.9 us (0.905)
  Pallas kernels: 23.1 us -> 20.7 us
    pallas_call x1, Pallas kernels: 23.1 us -> 20.7 us  [per_device(): pl.pallas_call(functools.partial(kernel, n, ns), out_shape=jax.ShapeDtype...]
where the time goes in v2:
time: 24.9 us; the launch traced here: 24.6 us
  Pallas kernels  20.7 us (83%)
  local copies, waits for them, and re-layouts  3.93 us (16%)
    pallas_call x1, Pallas kernels, per_device(): pl.pallas_call(functools.partial(kernel, n, ns), out_shape=jax.ShapeDtype...  20.7 us
    unnamed x9, local copies, waits for them, and re-layouts  3.93 us

profile of v2, /device:TPU:0, one launch (start us, length us, event | category | flops | bytes accessed | tf_op | source)
XLA Modules:
  0.0 24.6 jit_solution(7622639298878738484)
XLA Ops:
  0.0 0.0 copy-start.3
  0.0 0.7 %copy-done.3 = s32[1024]{0:T(1024)S(1)} copy-done((s32[1024]{0:T(1024)S(1)}, s32[1024]{0:T(1024)}, u32[]{:S(2)}) %copy-start.3) | copy-done | bytes 4120
  0.7 0.0 copy-start
  0.7 0.9 %copy-done = bf16[3,3,3,32,32]{4,3,2,1,0:T(8,128)(2,1)S(1)} copy-done((bf16[3,3,3,32,32]{4,3,2,1,0:T(8,128)(2,1)S(1)}, bf16[3,3,3,32,32]{4,3,2,1,0:T(8,128)(2,1)}, u32[]{:S(2)}) %copy-start) | copy-done | bytes 55320
  1.6 0.0 copy-start.1
  1.6 0.8 %copy-done.1 = bf16[1024,32]{0,1:T(8,128)(2,1)S(1)} copy-done((bf16[1024,32]{0,1:T(8,128)(2,1)S(1)}, bf16[1024,32]{0,1:T(8,128)(2,1)}, u32[]{:S(2)}) %copy-start.1) | copy-done | bytes 65560
  2.5 0.0 copy-start.2
  2.5 0.8 %copy-done.2 = bf16[1024,32]{0,1:T(8,128)(2,1)S(1)} copy-done((bf16[1024,32]{0,1:T(8,128)(2,1)S(1)}, bf16[1024,32]{0,1:T(8,128)(2,1)}, u32[]{:S(2)}) %copy-start.2) | copy-done | bytes 65560
  3.3 20.7 %shard_map.46 = bf16[32,1024]{1,0:T(8,128)(2,1)S(1)} custom-call(bf16[32,1024]{1,0:T(8,128)(2,1)S(1)} %bitcast.7, bf16[32,1024]{1,0:T(8,128)(2,1)S(1)} %bitcast.8, s32[4,1,256]{2,1,0:T(1,128)S(1)} %bitcast.9, bf16[864,32]{1,0:T(8,128)(2,1)S(1)} %bitcast.6), custom_call_target="tpu_custom_call" | custom-call | tf_op jit(solution)/shard_map/pallas_call | solution.py:337
  24.0 0.6 %copy.6 = bf16[1024,32]{0,1:T(8,128)(2,1)} copy(bf16[1024,32]{0,1:T(8,128)(2,1)S(1)} %bitcast.5) | data formatting | bytes 131072
Async XLA Ops:
  0.0 0.7 %copy-start.3 = (s32[1024]{0:T(1024)S(1)}, s32[1024]{0:T(1024)}, u32[]{:S(2)}) copy-start(s32[1024]{0:T(1024)} %param.5) | copy-start | bytes 12292
  0.7 0.9 %copy-start = (bf16[3,3,3,32,32]{4,3,2,1,0:T(8,128)(2,1)S(1)}, bf16[3,3,3,32,32]{4,3,2,1,0:T(8,128)(2,1)}, u32[]{:S(2)}) copy-start(bf16[3,3,3,32,32]{4,3,2,1,0:T(8,128)(2,1)} %param.7) | copy-start | bytes 165892
  1.6 0.8 %copy-start.1 = (bf16[1024,32]{0,1:T(8,128)(2,1)S(1)}, bf16[1024,32]{0,1:T(8,128)(2,1)}, u32[]{:S(2)}) copy-start(bf16[1024,32]{0,1:T(8,128)(2,1)} %param.4) | copy-start | bytes 196612
  2.5 0.8 %copy-start.2 = (bf16[1024,32]{0,1:T(8,128)(2,1)S(1)}, bf16[1024,32]{0,1:T(8,128)(2,1)}, u32[]{:S(2)}) copy-start(bf16[1024,32]{0,1:T(8,128)(2,1)} %param.6) | copy-start | bytes 196612

commit v3 on v2

--- a/solution.py
+++ b/solution.py
@@ -31,7 +31,7 @@
 def kernel(
     n, ns, feats, cots, vox, weights, out,
     gotf, gotc, gotv, w_in, hot, masked, sums, tiled, bmf, bef, bmb, beb,
-    inner, packed, hx, hc, hy, xm, xe, xh, acc, gy, div, back,
+    inner, packed, hx, hc, hy, xm, xe, xh, xs, acc, gy, div, back,
     local, fs, fr, cs, cr, vs, vr, hs, hr, rs, rr,
 ):
     s = lax.axis_index("space")
@@ -159,6 +159,8 @@
     for b in range(2):
         xm[b, 0:SIDE, :] = jnp.zeros((SIDE, 3 * HALF), BF16)
         xm[b, COLS + SIDE : COLS + 2 * SIDE, :] = jnp.zeros((SIDE, 3 * HALF), BF16)
+    xe[0, 0:SIDE, :] = jnp.zeros((SIDE, 3 * 128), BF16)
+    xe[0, COLS + SIDE : COLS + 2 * SIDE, :] = jnp.zeros((SIDE, 3 * 128), BF16)
 
     row = lax.broadcasted_iota(jnp.int32, (COLS, CAP), 0)
 
@@ -168,11 +170,18 @@
             r0 = q * LANES + x * C
             masked[d, r0 : r0 + C, :] = jnp.where(hi == x, val, 0.0).astype(BF16)
 
+    def pool_ones(d):
+        hot[d] = jnp.where(row == (gotv[d] & (COLS - 1)), 1.0, 0.0).astype(BF16)
+        mask(d, 1, 1.0)
+        term = nt(hot[d], masked[d, LANES : 2 * LANES, :])
+        if d == 0:
+            div[...] = term
+        else:
+            div[...] += term
+
     def pool_feats(d):
-        hot[d] = jnp.where(row == (gotv[d] & (COLS - 1)), 1.0, 0.0).astype(BF16)
         mask(d, 0, gotf[d].astype(F32))
-        mask(d, 1, 1.0)
-        term = nt(hot[d], masked[d, 0 : 2 * LANES, :])
+        term = nt(hot[d], masked[d, 0:LANES, :])
         if d == 0:
             sums[...] = term
         else:
@@ -186,15 +195,18 @@
         else:
             gy[...] += term
 
+    pool_ones(0)
     pool_feats(0)
     for d in range(1, n):
         copy_v(d).wait_recv()
+        pool_ones(d)
+    for d in range(1, n):
         copy_f(d).wait_recv()
         pool_feats(d)
 
-    count = jnp.maximum(sums[:, LANES:], 1.0)
+    count = jnp.maximum(div[...], 1.0)
     div[...] = count
-    mean = (sums[:, :LANES] / count).astype(BF16)
+    mean = (sums[...] / count).astype(BF16)
 
     def shifts(val):
         z = lax.broadcasted_iota(jnp.int32, val.shape, 0) & (SIDE - 1)
@@ -242,44 +254,58 @@
             @pl.when(exists(w))
             def _(k=k):
                 halo(p, k).start()
+        first = lax.broadcasted_iota(jnp.int32, (1, 128), 1) < C
+
+        def seam(v):
+            v = v[:, HALF - 128 : HALF + 128].astype(F32)
+            return jnp.where(first, v[:, 128:], v[:, :128])
+
         for b in range(2):
             for j, part in enumerate(shifts(val[:, b * HALF : (b + 1) * HALF].astype(F32))):
                 xm[b, SIDE : SIDE + COLS, j * HALF : (j + 1) * HALF] = part
-        total = None
+        for j, part in enumerate(shifts(seam(val))):
+            xe[0, SIDE : SIDE + COLS, j * 128 : (j + 1) * 128] = part
+        total, inside = None, None
         for dy in range(3):
-            lhs = xm[:, dy * SIDE : dy * SIDE + COLS, :].reshape(2 * COLS, 3 * HALF)
-            term = dot(lhs, main[dy])
+            at = slice(dy * SIDE, dy * SIDE + COLS)
+            term = dot(xm[:, at, :].reshape(2 * COLS, 3 * HALF), main[dy])
             total = term if total is None else total + term
+            term = dot(xe[0, at, :], edges[dy])
+            inside = term if inside is None else inside + term
         acc[...] = total.reshape(2, COLS, HALF)
+        acc[0, :, 128:] += inside[:, 128:]
+        acc[1, :, :128] += inside[:, :128]
         meanwhile()
         for k, w in enumerate(WAYS):
             @pl.when(exists((-w[0], -w[1])))
             def _(k=k):
                 halo(p, k).wait_recv()
         for side in range(2):
-            rim = hy[p, side].astype(F32)
+            rim = hy[p, side]
             for b in range(2):
-                for j, part in enumerate(shifts(rim[:, b * HALF : (b + 1) * HALF])):
+                for j, part in enumerate(shifts(rim[:, b * HALF : (b + 1) * HALF].astype(F32))):
                     xh[side, b, :, j * HALF : (j + 1) * HALF] = part
-        span = COLS + 2 * SIDE
-        first = lax.broadcasted_iota(jnp.int32, (span, 128), 1) < C
-        for b in range(2):
-            at = slice(HALF, HALF + 128) if b == 0 else slice(HALF - 128, HALF)
-            own = jnp.concatenate([hy[p, 0, :, at], inner[p, :, at], hy[p, 1, :, at]], axis=0).astype(F32)
-            far = jnp.concatenate(
+            for j, part in enumerate(shifts(seam(rim))):
+                xs[side, :, j * 128 : (j + 1) * 128] = part
+        left, right = (
+            jnp.concatenate(
                 [hc[p, b, 0].astype(F32), unpack(hx[p, b], 0 if b else 3), hc[p, b, 1].astype(F32)], axis=0)
-            edge = jnp.where(first, own, far) if b == 0 else jnp.where(first, far, own)
-            for j, part in enumerate(shifts(edge)):
-                xe[b, :, j * 128 : (j + 1) * 128] = part
+            for b in range(2))
+        for j, part in enumerate(shifts(jnp.where(first, right, left))):
+            xe[1, :, j * 128 : (j + 1) * 128] = part
         total = None
         for dy in range(3):
-            lhs = xe[:, dy * SIDE : dy * SIDE + COLS, :].reshape(2 * COLS, 3 * 128)
-            term = dot(lhs, edges[dy])
+            term = dot(xe[1, dy * SIDE : dy * SIDE + COLS, :], edges[dy])
             total = term if total is None else total + term
-        acc[...] += total.reshape(2, COLS, HALF)
+        acc[0, :, :128] += total[:, :128]
+        acc[1, :, 128:] += total[:, 128:]
         for side, dy, r0 in ((0, 0, 0), (1, 2, COLS - SIDE)):
+            at = slice(r0, r0 + SIDE)
             term = dot(xh[side].reshape(2 * SIDE, 3 * HALF), main[dy])
-            acc[:, r0 : r0 + SIDE, :] += term.reshape(2, SIDE, HALF)
+            acc[:, at, :] += term.reshape(2, SIDE, HALF)
+            term = dot(xs[side], edges[dy])
+            acc[0, at, 128:] += term[:, 128:]
+            acc[1, at, :128] += term[:, :128]
 
     def first_wait():
         for d in range(n):
@@ -346,7 +372,7 @@
             vm((27 * C, C), BF16),
             vm((n, COLS, CAP), BF16),
             vm((n, 3 * LANES, CAP), BF16),
-            vm((COLS, 2 * LANES), F32),
+            vm((COLS, LANES), F32),
             vm((27 * C, HALF), F32),
             vm((3, 3 * HALF, HALF), BF16),
             vm((3, 3 * 128, HALF), BF16),
@@ -360,6 +386,7 @@
             vm((2, span, 3 * HALF), BF16),
             vm((2, span, 3 * 128), BF16),
             vm((2, 2, SIDE, 3 * HALF), BF16),
+            vm((2, SIDE, 3 * 128), BF16),
             vm((2, COLS, HALF), F32),
             vm((COLS, LANES), F32),
             vm((COLS, LANES), F32),
@@ -368,7 +395,7 @@
             dma((2, 8)), dma((2, 8)), dma((n,)), dma((n,)),
         ],
         compiler_params=pltpu.CompilerParams(
-            collective_id=0, has_side_effects=True, vmem_limit_bytes=48 * 2**20
+            collective_id=0, has_side_effects=True, vmem_limit_bytes=63 * 2**20
         ),
     )(point_feats.T, cotangent.T, point_voxel.reshape(n, 1, CAP), weights.reshape(27 * C, C)).T
 

time: 24.9 us -> 22.1 us (0.89)
  local copies, waits for them, and re-layouts: 3.93 us -> 1.47 us
    unnamed x9 -> x1, local copies, waits for them, and re-layouts: 3.93 us -> 1.47 us
where the time goes in v3:
time: 22.1 us; the launch traced here: 22 us
  Pallas kernels  20.5 us (93%)
  local copies, waits for them, and re-layouts  1.47 us (7%)
    pallas_call x1, Pallas kernels, per_device(): pl.pallas_call(functools.partial(kernel, n, ns), out_shape=jax.ShapeDtype...  20.5 us
    unnamed x1, local copies, waits for them, and re-layouts  1.47 us

profile of v3, /device:TPU:0, one launch (start us, length us, event | category | flops | bytes accessed | tf_op | source)
XLA Modules:
  0.0 22.0 jit_solution(11110616121753183664)
XLA Ops:
  0.0 20.5 %shard_map.46 = bf16[32,1024]{1,0:T(8,128)(2,1)} custom-call(bf16[32,1024]{1,0:T(8,128)(2,1)} %bitcast.7, bf16[32,1024]{1,0:T(8,128)(2,1)} %bitcast.8, s32[4,1,256]{2,1,0:T(1,128)} %bitcast.9, bf16[864,32]{1,0:T(8,128)(2,1)} %bitcast.6), custom_call_target="tpu_custom_call" | custom-call | tf_op jit(solution)/shard_map/pallas_call | solution.py:363
  20.5 1.5 %copy.6 = bf16[1024,32]{0,1:T(8,128)(2,1)} copy(bf16[1024,32]{0,1:T(8,128)(2,1)} %bitcast.5) | data formatting | bytes 131072

commit v4 on v3

--- a/solution.py
+++ b/solution.py
@@ -70,6 +70,30 @@
         def _(w=w):
             pl.semaphore_signal(barrier, inc=1, device_id=(s + w[0], g + w[1]), device_id_type=MESH)
 
+    for p in range(2):
+        for side, d in ((0, -1), (1, 1)):
+            @pl.when(jnp.logical_not(exists((d, 0))))
+            def _(p=p, side=side):
+                hx[p, side] = jnp.zeros((COLS // 4, 128), BF16)
+
+            @pl.when(jnp.logical_not(exists((0, d))))
+            def _(p=p, side=side):
+                hy[p, side] = jnp.zeros((SIDE, LANES), BF16)
+
+            for side2, d2 in ((0, -1), (1, 1)):
+                @pl.when(jnp.logical_not(exists((d, d2))))
+                def _(p=p, side=side, side2=side2):
+                    hc[p, side, side2] = jnp.zeros((SIDE, 128), BF16)
+    for b in range(2):
+        xm[b, 0:SIDE, :] = jnp.zeros((SIDE, 3 * HALF), BF16)
+        xm[b, COLS + SIDE : COLS + 2 * SIDE, :] = jnp.zeros((SIDE, 3 * HALF), BF16)
+    xe[0, 0:SIDE, :] = jnp.zeros((SIDE, 3 * 128), BF16)
+    xe[0, COLS + SIDE : COLS + 2 * SIDE, :] = jnp.zeros((SIDE, 3 * 128), BF16)
+
+    for dy in range(3):
+        for dz in range(3):
+            bef[dy, dz * 128 + C : dz * 128 + 3 * C, :] = jnp.zeros((2 * C, HALF), BF16)
+
     peers = n - 1
     for w in outer:
         peers = peers + jnp.where(exists(w), 1, 0)
@@ -122,7 +146,6 @@
                 for i in range(wide):
                     bmf[dy, dz * HALF + i * C : dz * HALF + (i + 1) * C, :] = band(i, w0, w1, w2)
                 bef[dy, dz * 128 : dz * 128 + C, :] = jnp.where(block == wide - 1, w2, 0.0).astype(BF16)
-                bef[dy, dz * 128 + C : dz * 128 + 3 * C, :] = jnp.zeros((2 * C, HALF), BF16)
                 bef[dy, dz * 128 + 3 * C : dz * 128 + 4 * C, :] = jnp.where(block == 0, w0, 0.0).astype(BF16)
 
     def backward_bands():
@@ -142,26 +165,6 @@
 
     forward_bands()
 
-    for p in range(2):
-        for side, d in ((0, -1), (1, 1)):
-            @pl.when(jnp.logical_not(exists((d, 0))))
-            def _(p=p, side=side):
-                hx[p, side] = jnp.zeros((COLS // 4, 128), BF16)
-
-            @pl.when(jnp.logical_not(exists((0, d))))
-            def _(p=p, side=side):
-                hy[p, side] = jnp.zeros((SIDE, LANES), BF16)
-
-            for side2, d2 in ((0, -1), (1, 1)):
-                @pl.when(jnp.logical_not(exists((d, d2))))
-                def _(p=p, side=side, side2=side2):
-                    hc[p, side, side2] = jnp.zeros((SIDE, 128), BF16)
-    for b in range(2):
-        xm[b, 0:SIDE, :] = jnp.zeros((SIDE, 3 * HALF), BF16)
-        xm[b, COLS + SIDE : COLS + 2 * SIDE, :] = jnp.zeros((SIDE, 3 * HALF), BF16)
-    xe[0, 0:SIDE, :] = jnp.zeros((SIDE, 3 * 128), BF16)
-    xe[0, COLS + SIDE : COLS + 2 * SIDE, :] = jnp.zeros((SIDE, 3 * 128), BF16)
-
     row = lax.broadcasted_iota(jnp.int32, (COLS, CAP), 0)
 
     def mask(d, q, val):
@@ -200,13 +203,12 @@
     for d in range(1, n):
         copy_v(d).wait_recv()
         pool_ones(d)
+    div[...] = 1.0 / jnp.maximum(div[...], 1.0)
     for d in range(1, n):
         copy_f(d).wait_recv()
         pool_feats(d)
 
-    count = jnp.maximum(div[...], 1.0)
-    div[...] = count
-    mean = (sums[...] / count).astype(BF16)
+    inner[0] = (sums[...] * div[...]).astype(BF16)
 
     def shifts(val):
         z = lax.broadcasted_iota(jnp.int32, val.shape, 0) & (SIDE - 1)
@@ -246,8 +248,8 @@
             src_ref=src, dst_ref=dst, send_sem=hs.at[p, k], recv_sem=hr.at[p, k],
             device_id=(s + dx, g + dy), device_id_type=MESH)
 
-    def convolve(p, val, main, edges, dot, meanwhile):
-        inner[p] = val
+    def convolve(p, main, edges, dot, meanwhile):
+        val = inner[p]
         packed[p, 0] = pack(val[:, 0:128].astype(F32), 0)
         packed[p, 1] = pack(val[:, LANES - 128 :].astype(F32), 3)
         for k, w in enumerate(WAYS):
@@ -307,22 +309,31 @@
             acc[0, at, 128:] += term[:, 128:]
             acc[1, at, :128] += term[:, :128]
 
+    def gate(tile_no, rows):
+        at = slice(tile_no * 128, (tile_no + 1) * 128)
+        half = slice(tile_no % 2 * 128, (tile_no % 2 + 1) * 128)
+        o = acc[tile_no // 2, rows, half]
+        sig = 1.0 / (1.0 + jnp.exp(-o))
+        inner[1, rows, at] = (gy[rows, at] * sig * (1.0 + o * (1.0 - sig))).astype(BF16)
+
     def first_wait():
         for d in range(n):
             if d:
                 copy_c(d).wait_recv()
             pool_cots(d)
+        for tile_no in (1, 2):
+            gate(tile_no, slice(SIDE, COLS - SIDE))
         backward_bands()
 
-    convolve(0, mean, bmf, bef, nn, first_wait)
-    parts = []
-    for b in range(2):
-        o = acc[b]
-        sig = 1.0 / (1.0 + jnp.exp(-o))
-        parts.append((gy[:, b * HALF : (b + 1) * HALF] * sig * (1.0 + o * (1.0 - sig))).astype(BF16))
-    convolve(1, jnp.concatenate(parts, axis=1), bmb, beb, nt, lambda: None)
-
-    grad = jnp.concatenate([acc[b] / div[:, b * HALF : (b + 1) * HALF] for b in range(2)], axis=1)
+    convolve(0, bmf, bef, nn, first_wait)
+    for tile_no in (0, 3):
+        gate(tile_no, slice(0, COLS))
+    for tile_no in (1, 2):
+        gate(tile_no, slice(0, SIDE))
+        gate(tile_no, slice(COLS - SIDE, COLS))
+    convolve(1, bmb, beb, nt, lambda: None)
+
+    grad = jnp.concatenate([acc[b] * div[:, b * HALF : (b + 1) * HALF] for b in range(2)], axis=1)
     grad = jnp.transpose(grad).astype(BF16)
 
     def copy_r(d):
@@ -362,7 +373,7 @@
     dma = pltpu.SemaphoreType.DMA
     return pl.pallas_call(
         functools.partial(kernel, n, ns),
-        out_shape=jax.ShapeDtypeStruct((C, slots), BF16),
+        out_shape=pltpu.VMEM((C, slots), BF16),
         in_specs=[pl.BlockSpec(memory_space=pltpu.HBM)] * 4,
         out_specs=pl.BlockSpec(memory_space=vm),
         scratch_shapes=[

time: 22.1 us -> 20.7 us (0.937)
  local copies, waits for them, and re-layouts: 1.47 us -> 0.63 us
  Pallas kernels: 20.5 us -> 19.9 us
    unnamed x1, local copies, waits for them, and re-layouts: 1.47 us -> 0.63 us
    pallas_call x1, Pallas kernels: 20.5 us -> 19.9 us  [per_device(): pl.pallas_call(functools.partial(kernel, n, ns), out_shape=pltpu.VMEM((C,...]
where the time goes in v4:
time: 20.7 us; the launch traced here: 20.5 us
  Pallas kernels  19.9 us (96%)
  local copies, waits for them, and re-layouts  0.63 us (3%)
    pallas_call x1, Pallas kernels, per_device(): pl.pallas_call(functools.partial(kernel, n, ns), out_shape=pltpu.VMEM((C,...  19.9 us
    unnamed x1, local copies, waits for them, and re-layouts  0.63 us

profile of v4, /device:TPU:0, one launch (start us, length us, event | category | flops | bytes accessed | tf_op | source)
XLA Modules:
  0.0 20.5 jit_solution(11192477900445076581)
XLA Ops:
  0.0 19.9 %shard_map.46 = bf16[32,1024]{1,0:T(8,128)(2,1)S(1)} custom-call(bf16[32,1024]{1,0:T(8,128)(2,1)} %bitcast.7, bf16[32,1024]{1,0:T(8,128)(2,1)} %bitcast.8, s32[4,1,256]{2,1,0:T(1,128)} %bitcast.9, bf16[864,32]{1,0:T(8,128)(2,1)} %bitcast.6), custom_call_target="tpu_custom_call" | custom-call | tf_op jit(solution)/shard_map/pallas_call | solution.py:374
  19.9 0.6 %copy.6 = bf16[1024,32]{0,1:T(8,128)(2,1)} copy(bf16[1024,32]{0,1:T(8,128)(2,1)S(1)} %bitcast.5) | data formatting | bytes 131072

commit v5 on v4

--- a/solution.py
+++ b/solution.py
@@ -31,7 +31,7 @@
 def kernel(
     n, ns, feats, cots, vox, weights, out,
     gotf, gotc, gotv, w_in, hot, masked, sums, tiled, bmf, bef, bmb, beb,
-    inner, packed, hx, hc, hy, xm, xe, xh, xs, acc, gy, div, back,
+    inner, packed, hx, hc, hy, xm, xe, xh, xf, acc, gy, div, back,
     local, fs, fr, cs, cr, vs, vr, hs, hr, rs, rr,
 ):
     s = lax.axis_index("space")
@@ -87,8 +87,8 @@
     for b in range(2):
         xm[b, 0:SIDE, :] = jnp.zeros((SIDE, 3 * HALF), BF16)
         xm[b, COLS + SIDE : COLS + 2 * SIDE, :] = jnp.zeros((SIDE, 3 * HALF), BF16)
-    xe[0, 0:SIDE, :] = jnp.zeros((SIDE, 3 * 128), BF16)
-    xe[0, COLS + SIDE : COLS + 2 * SIDE, :] = jnp.zeros((SIDE, 3 * 128), BF16)
+    xe[0:SIDE, :] = jnp.zeros((SIDE, 3 * 128), BF16)
+    xe[COLS + SIDE : COLS + 2 * SIDE, :] = jnp.zeros((SIDE, 3 * 128), BF16)
 
     for dy in range(3):
         for dz in range(3):
@@ -167,48 +167,31 @@
 
     row = lax.broadcasted_iota(jnp.int32, (COLS, CAP), 0)
 
+    def columns(d):
+        return slice(d * CAP, (d + 1) * CAP)
+
     def mask(d, q, val):
         hi = jnp.broadcast_to(gotv[d] >> 8, (C, CAP))
         for x in range(SIDE):
             r0 = q * LANES + x * C
-            masked[d, r0 : r0 + C, :] = jnp.where(hi == x, val, 0.0).astype(BF16)
-
-    def pool_ones(d):
-        hot[d] = jnp.where(row == (gotv[d] & (COLS - 1)), 1.0, 0.0).astype(BF16)
+            masked[r0 : r0 + C, columns(d)] = jnp.where(hi == x, val, 0.0).astype(BF16)
+
+    def ones(d):
+        hot[:, columns(d)] = jnp.where(row == (gotv[d] & (COLS - 1)), 1.0, 0.0).astype(BF16)
         mask(d, 1, 1.0)
-        term = nt(hot[d], masked[d, LANES : 2 * LANES, :])
-        if d == 0:
-            div[...] = term
-        else:
-            div[...] += term
-
-    def pool_feats(d):
+
+    ones(0)
+    mask(0, 0, gotf[0].astype(F32))
+    sums[...] = nt(hot[:, columns(0)], masked[0:LANES, columns(0)])
+    for d in range(1, n):
+        copy_v(d).wait_recv()
+        ones(d)
+    div[...] = 1.0 / jnp.maximum(nt(hot[...], masked[LANES : 2 * LANES, :]), 1.0)
+    for d in range(1, n):
+        copy_f(d).wait_recv()
         mask(d, 0, gotf[d].astype(F32))
-        term = nt(hot[d], masked[d, 0:LANES, :])
-        if d == 0:
-            sums[...] = term
-        else:
-            sums[...] += term
-
-    def pool_cots(d):
-        mask(d, 2, gotc[d].astype(F32))
-        term = nt(hot[d], masked[d, 2 * LANES :, :])
-        if d == 0:
-            gy[...] = term
-        else:
-            gy[...] += term
-
-    pool_ones(0)
-    pool_feats(0)
-    for d in range(1, n):
-        copy_v(d).wait_recv()
-        pool_ones(d)
-    div[...] = 1.0 / jnp.maximum(div[...], 1.0)
-    for d in range(1, n):
-        copy_f(d).wait_recv()
-        pool_feats(d)
-
-    inner[0] = (sums[...] * div[...]).astype(BF16)
+    far_sums = nt(hot[:, CAP:], masked[0:LANES, CAP:])
+    inner[0] = ((sums[...] + far_sums) * div[...]).astype(BF16)
 
     def shifts(val):
         z = lax.broadcasted_iota(jnp.int32, val.shape, 0) & (SIDE - 1)
@@ -248,7 +231,7 @@
             src_ref=src, dst_ref=dst, send_sem=hs.at[p, k], recv_sem=hr.at[p, k],
             device_id=(s + dx, g + dy), device_id_type=MESH)
 
-    def convolve(p, main, edges, dot, meanwhile):
+    def convolve(p, main, edges, dot, before, meanwhile):
         val = inner[p]
         packed[p, 0] = pack(val[:, 0:128].astype(F32), 0)
         packed[p, 1] = pack(val[:, LANES - 128 :].astype(F32), 3)
@@ -256,6 +239,7 @@
             @pl.when(exists(w))
             def _(k=k):
                 halo(p, k).start()
+        before()
         first = lax.broadcasted_iota(jnp.int32, (1, 128), 1) < C
 
         def seam(v):
@@ -266,13 +250,13 @@
             for j, part in enumerate(shifts(val[:, b * HALF : (b + 1) * HALF].astype(F32))):
                 xm[b, SIDE : SIDE + COLS, j * HALF : (j + 1) * HALF] = part
         for j, part in enumerate(shifts(seam(val))):
-            xe[0, SIDE : SIDE + COLS, j * 128 : (j + 1) * 128] = part
+            xe[SIDE : SIDE + COLS, j * 128 : (j + 1) * 128] = part
         total, inside = None, None
         for dy in range(3):
             at = slice(dy * SIDE, dy * SIDE + COLS)
             term = dot(xm[:, at, :].reshape(2 * COLS, 3 * HALF), main[dy])
             total = term if total is None else total + term
-            term = dot(xe[0, at, :], edges[dy])
+            term = dot(xe[at, :], edges[dy])
             inside = term if inside is None else inside + term
         acc[...] = total.reshape(2, COLS, HALF)
         acc[0, :, 128:] += inside[:, 128:]
@@ -288,26 +272,25 @@
                 for j, part in enumerate(shifts(rim[:, b * HALF : (b + 1) * HALF].astype(F32))):
                     xh[side, b, :, j * HALF : (j + 1) * HALF] = part
             for j, part in enumerate(shifts(seam(rim))):
-                xs[side, :, j * 128 : (j + 1) * 128] = part
+                r0 = side * (COLS + 3 * SIDE)
+                xf[r0 : r0 + SIDE, j * 128 : (j + 1) * 128] = part
         left, right = (
             jnp.concatenate(
                 [hc[p, b, 0].astype(F32), unpack(hx[p, b], 0 if b else 3), hc[p, b, 1].astype(F32)], axis=0)
             for b in range(2))
         for j, part in enumerate(shifts(jnp.where(first, right, left))):
-            xe[1, :, j * 128 : (j + 1) * 128] = part
-        total = None
-        for dy in range(3):
-            term = dot(xe[1, dy * SIDE : dy * SIDE + COLS, :], edges[dy])
-            total = term if total is None else total + term
+            xf[SIDE : COLS + 3 * SIDE, j * 128 : (j + 1) * 128] = part
+        upper = dot(xf[0 : COLS + SIDE, :], edges[0])
+        lower = dot(xf[3 * SIDE : COLS + 4 * SIDE, :], edges[2])
+        total = upper[SIDE:] + dot(xf[2 * SIDE : COLS + 2 * SIDE, :], edges[1]) + lower[:COLS]
         acc[0, :, :128] += total[:, :128]
         acc[1, :, 128:] += total[:, 128:]
-        for side, dy, r0 in ((0, 0, 0), (1, 2, COLS - SIDE)):
+        for side, dy, r0, rim in ((0, 0, 0, upper[:SIDE]), (1, 2, COLS - SIDE, lower[COLS:])):
             at = slice(r0, r0 + SIDE)
             term = dot(xh[side].reshape(2 * SIDE, 3 * HALF), main[dy])
             acc[:, at, :] += term.reshape(2, SIDE, HALF)
-            term = dot(xs[side], edges[dy])
-            acc[0, at, 128:] += term[:, 128:]
-            acc[1, at, :128] += term[:, :128]
+            acc[0, at, 128:] += rim[:, 128:]
+            acc[1, at, :128] += rim[:, :128]
 
     def gate(tile_no, rows):
         at = slice(tile_no * 128, (tile_no + 1) * 128)
@@ -320,18 +303,18 @@
         for d in range(n):
             if d:
                 copy_c(d).wait_recv()
-            pool_cots(d)
+            mask(d, 2, gotc[d].astype(F32))
+        gy[...] = nt(hot[...], masked[2 * LANES :, :])
         for tile_no in (1, 2):
             gate(tile_no, slice(SIDE, COLS - SIDE))
-        backward_bands()
-
-    convolve(0, bmf, bef, nn, first_wait)
+
+    convolve(0, bmf, bef, nn, lambda: None, first_wait)
     for tile_no in (0, 3):
         gate(tile_no, slice(0, COLS))
     for tile_no in (1, 2):
         gate(tile_no, slice(0, SIDE))
         gate(tile_no, slice(COLS - SIDE, COLS))
-    convolve(1, bmb, beb, nt, lambda: None)
+    convolve(1, bmb, beb, nt, backward_bands, lambda: None)
 
     grad = jnp.concatenate([acc[b] * div[:, b * HALF : (b + 1) * HALF] for b in range(2)], axis=1)
     grad = jnp.transpose(grad).astype(BF16)
@@ -343,7 +326,7 @@
 
     for d in list(range(1, n)) + [0]:
         hi = jnp.broadcast_to(gotv[d] >> 8, (C, CAP))
-        rows = nn(grad, hot[d])
+        rows = nn(grad, hot[:, columns(d)])
         picked = jnp.zeros((C, CAP), F32)
         for x in range(SIDE):
             picked = picked + jnp.where(hi == x, rows[x * C : (x + 1) * C], 0.0)
@@ -381,8 +364,8 @@
             vm((n, C, CAP), BF16),
             vm((n, 1, CAP), jnp.int32),
             vm((27 * C, C), BF16),
-            vm((n, COLS, CAP), BF16),
-            vm((n, 3 * LANES, CAP), BF16),
+            vm((COLS, slots), BF16),
+            vm((3 * LANES, slots), BF16),
             vm((COLS, LANES), F32),
             vm((27 * C, HALF), F32),
             vm((3, 3 * HALF, HALF), BF16),
@@ -395,9 +378,9 @@
             vm((2, 2, 2, SIDE, 128), BF16),
             vm((2, 2, SIDE, LANES), BF16),
             vm((2, span, 3 * HALF), BF16),
-            vm((2, span, 3 * 128), BF16),
+            vm((span, 3 * 128), BF16),
             vm((2, 2, SIDE, 3 * HALF), BF16),
-            vm((2, SIDE, 3 * 128), BF16),
+            vm((span + 2 * SIDE, 3 * 128), BF16),
             vm((2, COLS, HALF), F32),
             vm((COLS, LANES), F32),
             vm((COLS, LANES), F32),

time: 20.7 us -> 20.7 us (level)
  no operation moved by 1% of the time
where the time goes in v5:
time: 20.7 us; the launch traced here: 20.6 us
  Pallas kernels  19.9 us (96%)
  local copies, waits for them, and re-layouts  0.63 us (3%)
    pallas_call x1, Pallas kernels, per_device(): pl.pallas_call(functools.partial(kernel, n, ns), out_shape=pltpu.VMEM((C,...  19.9 us
    unnamed x1, local copies, waits for them, and re-layouts  0.63 us

profile of v5, /device:TPU:0, one launch (start us, length us, event | category | flops | bytes accessed | tf_op | source)
XLA Modules:
  0.0 20.6 jit_solution(904424255972238987)
XLA Ops:
  0.0 19.9 %shard_map.46 = bf16[32,1024]{1,0:T(8,128)(2,1)S(1)} custom-call(bf16[32,1024]{1,0:T(8,128)(2,1)} %bitcast.7, bf16[32,1024]{1,0:T(8,128)(2,1)} %bitcast.8, s32[4,1,256]{2,1,0:T(1,128)} %bitcast.9, bf16[864,32]{1,0:T(8,128)(2,1)} %bitcast.6), custom_call_target="tpu_custom_call" | custom-call | tf_op jit(solution)/shard_map/pallas_call | solution.py:357
  19.9 0.6 %copy.6 = bf16[1024,32]{0,1:T(8,128)(2,1)} copy(bf16[1024,32]{0,1:T(8,128)(2,1)S(1)} %bitcast.5) | data formatting | bytes 131072

commit v6 on v5

--- a/solution.py
+++ b/solution.py
@@ -19,6 +19,8 @@
 
 WAYS = ((-1, 0), (1, 0), (0, -1), (0, 1), (-1, -1), (-1, 1), (1, -1), (1, 1))
 
+BANDS = tuple((i, h) for i in range(8) for h in range(2) if any(0 <= x < 8 and x // 4 == h for x in (i - 1, i, i + 1)))
+
 
 def nt(a, b):
     return lax.dot_general(a, b, (((1,), (1,)), ((), ())), preferred_element_type=F32)
@@ -30,7 +32,7 @@
 
 def kernel(
     n, ns, feats, cots, vox, weights, out,
-    gotf, gotc, gotv, w_in, hot, masked, sums, tiled, bmf, bef, bmb, beb,
+    gotf, gotc, gotv, w_in, hot, masked, sums, tiled, bmf, bef, beb,
     inner, packed, hx, hc, hy, xm, xe, xh, xf, acc, gy, div, back,
     local, fs, fr, cs, cr, vs, vr, hs, hr, rs, rr,
 ):
@@ -92,7 +94,14 @@
 
     for dy in range(3):
         for dz in range(3):
-            bef[dy, dz * 128 + C : dz * 128 + 3 * C, :] = jnp.zeros((2 * C, HALF), BF16)
+            for i in range(HALF // C):
+                for h in range(2):
+                    if (i, h) not in BANDS:
+                        bmf[dy, dz * HALF + i * C : dz * HALF + (i + 1) * C, h * 128 : (h + 1) * 128] = jnp.zeros(
+                            (C, 128), BF16)
+            bef[dy, dz * 128 : (dz + 1) * 128, :128] = jnp.zeros((128, 128), BF16)
+            bef[dy, dz * 128 : (dz + 1) * 128, 128:] = jnp.zeros((128, 128), BF16)
+            beb[dy, C : HALF - C, dz * 128 : (dz + 1) * 128] = jnp.zeros((HALF - 2 * C, 128), BF16)
 
     peers = n - 1
     for w in outer:
@@ -122,48 +131,31 @@
     for c in own_copies:
         c.wait()
 
+    block = lax.broadcasted_iota(jnp.int32, (C, 128), 1) // C
     spread = jnp.where(
-        (lax.broadcasted_iota(jnp.int32, (C, HALF), 1) & (C - 1)) == lax.broadcasted_iota(jnp.int32, (C, HALF), 0),
+        (lax.broadcasted_iota(jnp.int32, (C, 128), 1) & (C - 1)) == lax.broadcasted_iota(jnp.int32, (C, 128), 0),
         1.0, 0.0).astype(BF16)
     tiled[...] = nn(w_in[...], spread)
-    block = lax.broadcasted_iota(jnp.int32, (C, HALF), 1) // C
-    narrow = lax.broadcasted_iota(jnp.int32, (C, 128), 1) // C
-    none = jnp.zeros((C, 128), BF16)
-    wide = HALF // C
 
     def tile(dx, dy, dz):
         a = (dx * 3 + dy) * 3 + dz
         return tiled[a * C : (a + 1) * C, :]
 
-    def band(i, w0, w1, w2):
-        inside = jnp.where(block == i, w1, jnp.where(block == i - 1, w2, jnp.where(block == i + 1, w0, 0.0)))
-        return inside.astype(BF16)
-
-    def forward_bands():
-        for dy in range(3):
-            for dz in range(3):
-                w0, w1, w2 = (tile(dx, dy, dz) for dx in range(3))
-                for i in range(wide):
-                    bmf[dy, dz * HALF + i * C : dz * HALF + (i + 1) * C, :] = band(i, w0, w1, w2)
-                bef[dy, dz * 128 : dz * 128 + C, :] = jnp.where(block == wide - 1, w2, 0.0).astype(BF16)
-                bef[dy, dz * 128 + 3 * C : dz * 128 + 4 * C, :] = jnp.where(block == 0, w0, 0.0).astype(BF16)
-
-    def backward_bands():
-        for fy in range(3):
-            for fz in range(3):
-                w0, w1, w2 = (tile(dx, 2 - fy, 2 - fz) for dx in range(3))
-                for i in range(wide):
-                    at = slice(i * C, (i + 1) * C)
-                    bmb[fy, at, fz * HALF : (fz + 1) * HALF] = band(i, w0, w1, w2)
-                    if i == wide - 1:
-                        edge = jnp.where(narrow == 0, w0[:, :128], 0.0).astype(BF16)
-                    elif i == 0:
-                        edge = jnp.where(narrow == 3, w2[:, :128], 0.0).astype(BF16)
-                    else:
-                        edge = none
-                    beb[fy, at, fz * 128 : (fz + 1) * 128] = edge
-
-    forward_bands()
+    for dy in range(3):
+        for dz in range(3):
+            w0, w1, w2 = (tile(dx, dy, dz) for dx in range(3))
+            for i, h in BANDS:
+                piece = 0.0
+                for at, w in ((i + 1, w0), (i - 1, w2), (i, w1)):
+                    if at // 4 == h:
+                        piece = jnp.where(block == at % 4, w, piece)
+                bmf[dy, dz * HALF + i * C : dz * HALF + (i + 1) * C, h * 128 : (h + 1) * 128] = piece.astype(BF16)
+            high, low = jnp.where(block == 3, w2, 0.0).astype(BF16), jnp.where(block == 0, w0, 0.0).astype(BF16)
+            bef[dy, dz * 128 : dz * 128 + C, 128:] = high
+            bef[dy, dz * 128 + 3 * C : dz * 128 + 4 * C, :128] = low
+            at = slice((2 - dz) * 128, (3 - dz) * 128)
+            beb[2 - dy, HALF - C :, at] = low
+            beb[2 - dy, 0:C, at] = high
 
     row = lax.broadcasted_iota(jnp.int32, (COLS, CAP), 0)
 
@@ -231,7 +223,7 @@
             src_ref=src, dst_ref=dst, send_sem=hs.at[p, k], recv_sem=hr.at[p, k],
             device_id=(s + dx, g + dy), device_id_type=MESH)
 
-    def convolve(p, main, edges, dot, before, meanwhile):
+    def convolve(p, main, edges, dot, meanwhile):
         val = inner[p]
         packed[p, 0] = pack(val[:, 0:128].astype(F32), 0)
         packed[p, 1] = pack(val[:, LANES - 128 :].astype(F32), 3)
@@ -239,7 +231,6 @@
             @pl.when(exists(w))
             def _(k=k):
                 halo(p, k).start()
-        before()
         first = lax.broadcasted_iota(jnp.int32, (1, 128), 1) < C
 
         def seam(v):
@@ -254,7 +245,7 @@
         total, inside = None, None
         for dy in range(3):
             at = slice(dy * SIDE, dy * SIDE + COLS)
-            term = dot(xm[:, at, :].reshape(2 * COLS, 3 * HALF), main[dy])
+            term = main(xm[:, at, :].reshape(2 * COLS, 3 * HALF), dy)
             total = term if total is None else total + term
             term = dot(xe[at, :], edges[dy])
             inside = term if inside is None else inside + term
@@ -287,7 +278,7 @@
         acc[1, :, 128:] += total[:, 128:]
         for side, dy, r0, rim in ((0, 0, 0, upper[:SIDE]), (1, 2, COLS - SIDE, lower[COLS:])):
             at = slice(r0, r0 + SIDE)
-            term = dot(xh[side].reshape(2 * SIDE, 3 * HALF), main[dy])
+            term = main(xh[side].reshape(2 * SIDE, 3 * HALF), dy)
             acc[:, at, :] += term.reshape(2, SIDE, HALF)
             acc[0, at, 128:] += rim[:, 128:]
             acc[1, at, :128] += rim[:, :128]
@@ -298,6 +289,17 @@
         o = acc[tile_no // 2, rows, half]
         sig = 1.0 / (1.0 + jnp.exp(-o))
         inner[1, rows, at] = (gy[rows, at] * sig * (1.0 + o * (1.0 - sig))).astype(BF16)
+
+    def forward(lhs, dy):
+        return nn(lhs, bmf[dy])
+
+    def backward(lhs, dy):
+        total = None
+        for dz in range(3):
+            flip = slice((2 - dz) * HALF, (3 - dz) * HALF)
+            term = nt(lhs[:, dz * HALF : (dz + 1) * HALF], bmf[2 - dy, flip, :])
+            total = term if total is None else total + term
+        return total
 
     def first_wait():
         for d in range(n):
@@ -308,13 +310,13 @@
         for tile_no in (1, 2):
             gate(tile_no, slice(SIDE, COLS - SIDE))
 
-    convolve(0, bmf, bef, nn, lambda: None, first_wait)
+    convolve(0, forward, bef, nn, first_wait)
     for tile_no in (0, 3):
         gate(tile_no, slice(0, COLS))
     for tile_no in (1, 2):
         gate(tile_no, slice(0, SIDE))
         gate(tile_no, slice(COLS - SIDE, COLS))
-    convolve(1, bmb, beb, nt, backward_bands, lambda: None)
+    convolve(1, backward, beb, nt, lambda: None)
 
     grad = jnp.concatenate([acc[b] * div[:, b * HALF : (b + 1) * HALF] for b in range(2)], axis=1)
     grad = jnp.transpose(grad).astype(BF16)
@@ -336,17 +338,16 @@
             back[d] = picked.astype(BF16)
             copy_r(d).start()
     for d in range(1, n):
-        copy_r(d).wait_recv()
-    for d in range(1, n):
         copy_v(d).wait_send()
         copy_f(d).wait_send()
         copy_c(d).wait_send()
-        copy_r(d).wait_send()
     for p in range(2):
         for k, w in enumerate(WAYS):
             @pl.when(exists(w))
             def _(p=p, k=k):
                 halo(p, k).wait_send()
+    for d in range(1, n):
+        copy_r(d).wait()
 
 
 def per_device(n, ns, point_feats, point_voxel, cotangent, weights):
@@ -367,10 +368,9 @@
             vm((COLS, slots), BF16),
             vm((3 * LANES, slots), BF16),
             vm((COLS, LANES), F32),
-            vm((27 * C, HALF), F32),
+            vm((27 * C, 128), F32),
             vm((3, 3 * HALF, HALF), BF16),
             vm((3, 3 * 128, HALF), BF16),
-            vm((3, HALF, 3 * HALF), BF16),
             vm((3, HALF, 3 * 128), BF16),
             vm((2, COLS, LANES), BF16),
             vm((2, 2, COLS // 4, 128), BF16),

time: 20.7 us -> 20.5 us (level)
  no operation moved by 1% of the time
where the time goes in v6:
time: 20.5 us; the launch traced here: 20.4 us
  Pallas kernels  19.7 us (96%)
  local copies, waits for them, and re-layouts  0.63 us (3%)
    pallas_call x1, Pallas kernels, per_device(): pl.pallas_call(functools.partial(kernel, n, ns), out_shape=pltpu.VMEM((C,...  19.7 us
    unnamed x1, local copies, waits for them, and re-layouts  0.63 us

profile of v6, /device:TPU:0, one launch (start us, length us, event | category | flops | bytes accessed | tf_op | source)
XLA Modules:
  0.0 20.4 jit_solution(14865910216346334620)
XLA Ops:
  0.0 19.7 %shard_map.46 = bf16[32,1024]{1,0:T(8,128)(2,1)S(1)} custom-call(bf16[32,1024]{1,0:T(8,128)(2,1)} %bitcast.7, bf16[32,1024]{1,0:T(8,128)(2,1)} %bitcast.8, s32[4,1,256]{2,1,0:T(1,128)} %bitcast.9, bf16[864,32]{1,0:T(8,128)(2,1)} %bitcast.6), custom_call_target="tpu_custom_call" | custom-call | tf_op jit(solution)/shard_map/pallas_call | solution.py:358
  19.7 0.6 %copy.6 = bf16[1024,32]{0,1:T(8,128)(2,1)} copy(bf16[1024,32]{0,1:T(8,128)(2,1)S(1)} %bitcast.5) | data formatting | bytes 131072

commit v7 on v6

--- a/solution.py
+++ b/solution.py
@@ -17,7 +17,7 @@
 HALF = LANES // 2
 CAP = 256
 
-WAYS = ((-1, 0), (1, 0), (0, -1), (0, 1), (-1, -1), (-1, 1), (1, -1), (1, 1))
+WAYS = ((-1, -1), (-1, 1), (1, -1), (1, 1), (-1, 0), (1, 0), (0, -1), (0, 1))
 
 BANDS = tuple((i, h) for i in range(8) for h in range(2) if any(0 <= x < 8 and x // 4 == h for x in (i - 1, i, i + 1)))
 
@@ -225,9 +225,11 @@
 
     def convolve(p, main, edges, dot, meanwhile):
         val = inner[p]
-        packed[p, 0] = pack(val[:, 0:128].astype(F32), 0)
-        packed[p, 1] = pack(val[:, LANES - 128 :].astype(F32), 3)
         for k, w in enumerate(WAYS):
+            if k == 4:
+                packed[p, 0] = pack(val[:, 0:128].astype(F32), 0)
+                packed[p, 1] = pack(val[:, LANES - 128 :].astype(F32), 3)
+
             @pl.when(exists(w))
             def _(k=k):
                 halo(p, k).start()
@@ -242,16 +244,23 @@
                 xm[b, SIDE : SIDE + COLS, j * HALF : (j + 1) * HALF] = part
         for j, part in enumerate(shifts(seam(val))):
             xe[SIDE : SIDE + COLS, j * 128 : (j + 1) * 128] = part
-        total, inside = None, None
-        for dy in range(3):
-            at = slice(dy * SIDE, dy * SIDE + COLS)
-            term = main(xm[:, at, :].reshape(2 * COLS, 3 * HALF), dy)
-            total = term if total is None else total + term
-            term = dot(xe[at, :], edges[dy])
-            inside = term if inside is None else inside + term
-        acc[...] = total.reshape(2, COLS, HALF)
-        acc[0, :, 128:] += inside[:, 128:]
-        acc[1, :, :128] += inside[:, :128]
+        def row_step(dy, first_step):
+            at = pl.ds(pl.multiple_of(dy * SIDE, SIDE), COLS)
+            term = main(xm[:, at, :].reshape(2 * COLS, 3 * HALF), dy).reshape(2, COLS, HALF)
+            inside = dot(xe[at, :], edges[dy])
+            if first_step:
+                acc[...] = term
+            else:
+                acc[...] += term
+            acc[0, :, 128:] += inside[:, 128:]
+            acc[1, :, :128] += inside[:, :128]
+
+        row_step(0, True)
+
+        @pl.loop(1, 3)
+        def _(dy):
+            row_step(dy, False)
+
         meanwhile()
         for k, w in enumerate(WAYS):
             @pl.when(exists((-w[0], -w[1])))
@@ -326,17 +335,20 @@
             src_ref=back.at[d], dst_ref=out.at[:, slots_of(g)], send_sem=rs.at[d], recv_sem=rr.at[d],
             device_id=(s, peer(n - d)), device_id_type=MESH)
 
-    for d in list(range(1, n)) + [0]:
+    def picked(d):
         hi = jnp.broadcast_to(gotv[d] >> 8, (C, CAP))
-        rows = nn(grad, hot[:, columns(d)])
-        picked = jnp.zeros((C, CAP), F32)
+        rows = nn(grad, hot[:, slots_of(d)])
+        total = jnp.zeros((C, CAP), F32)
         for x in range(SIDE):
-            picked = picked + jnp.where(hi == x, rows[x * C : (x + 1) * C], 0.0)
-        if d == 0:
-            out[:, slots_of(g)] = picked.astype(BF16)
-        else:
-            back[d] = picked.astype(BF16)
-            copy_r(d).start()
+            total = total + jnp.where(hi == x, rows[x * C : (x + 1) * C], 0.0)
+        return total.astype(BF16)
+
+    @pl.loop(1, n)
+    def _(d):
+        back[d] = picked(d)
+        copy_r(d).start()
+
+    out[:, slots_of(g)] = picked(0)
     for d in range(1, n):
         copy_v(d).wait_send()
         copy_f(d).wait_send()

time: 20.5 us -> 20.1 us (0.980)
  Pallas kernels: 19.7 us -> 19.3 us
    pallas_call x1, Pallas kernels: 19.7 us -> 19.3 us  [per_device(): pl.pallas_call(functools.partial(kernel, n, ns), out_shape=pltpu.VMEM((C,...]
where the time goes in v7:
time: 20.1 us; the launch traced here: 19.9 us
  Pallas kernels  19.3 us (96%)
  local copies, waits for them, and re-layouts  0.63 us (3%)
    pallas_call x1, Pallas kernels, per_device(): pl.pallas_call(functools.partial(kernel, n, ns), out_shape=pltpu.VMEM((C,...  19.3 us
    unnamed x1, local copies, waits for them, and re-layouts  0.63 us

profile of v7, /device:TPU:0, one launch (start us, length us, event | category | flops | bytes accessed | tf_op | source)
XLA Modules:
  0.0 19.9 jit_solution(18328948497564737886)
XLA Ops:
  0.0 19.3 %shard_map.46 = bf16[32,1024]{1,0:T(8,128)(2,1)S(1)} custom-call(bf16[32,1024]{1,0:T(8,128)(2,1)} %bitcast.7, bf16[32,1024]{1,0:T(8,128)(2,1)} %bitcast.8, s32[4,1,256]{2,1,0:T(1,128)} %bitcast.9, bf16[864,32]{1,0:T(8,128)(2,1)} %bitcast.6), custom_call_target="tpu_custom_call" | custom-call | tf_op jit(solution)/shard_map/pallas_call | solution.py:370
  19.3 0.6 %copy.6 = bf16[1024,32]{0,1:T(8,128)(2,1)} copy(bf16[1024,32]{0,1:T(8,128)(2,1)S(1)} %bitcast.5) | data formatting | bytes 131072

commit v8 on v7

--- a/solution.py
+++ b/solution.py
@@ -18,6 +18,8 @@
 CAP = 256
 
 WAYS = ((-1, -1), (-1, 1), (1, -1), (1, 1), (-1, 0), (1, 0), (0, -1), (0, 1))
+
+OUTER_FIRST = (0, 1, 2, 3, 12, 13, 14, 15, 4, 5, 6, 7, 8, 9, 10, 11)
 
 BANDS = tuple((i, h) for i in range(8) for h in range(2) if any(0 <= x < 8 and x // 4 == h for x in (i - 1, i, i + 1)))
 
@@ -123,10 +125,11 @@
             src_ref=cots.at[:, slots_of(peer(d))], dst_ref=gotc.at[d], send_sem=cs.at[d], recv_sem=cr.at[d],
             device_id=(s, peer(d)), device_id_type=MESH)
 
-    for d in range(1, n):
+    far_first = sorted(range(1, n), key=lambda d: -min(d, n - d))
+    for d in far_first:
         copy_v(d).start()
         copy_f(d).start()
-    for d in range(1, n):
+    for d in far_first:
         copy_c(d).start()
     for c in own_copies:
         c.wait()
@@ -165,7 +168,7 @@
     def mask(d, q, val):
         hi = jnp.broadcast_to(gotv[d] >> 8, (C, CAP))
         for x in range(SIDE):
-            r0 = q * LANES + x * C
+            r0 = q * LANES + (x if q else OUTER_FIRST.index(x)) * C
             masked[r0 : r0 + C, columns(d)] = jnp.where(hi == x, val, 0.0).astype(BF16)
 
     def ones(d):
@@ -182,8 +185,6 @@
     for d in range(1, n):
         copy_f(d).wait_recv()
         mask(d, 0, gotf[d].astype(F32))
-    far_sums = nt(hot[:, CAP:], masked[0:LANES, CAP:])
-    inner[0] = ((sums[...] + far_sums) * div[...]).astype(BF16)
 
     def shifts(val):
         z = lax.broadcasted_iota(jnp.int32, val.shape, 0) & (SIDE - 1)
@@ -223,16 +224,21 @@
             src_ref=src, dst_ref=dst, send_sem=hs.at[p, k], recv_sem=hr.at[p, k],
             device_id=(s + dx, g + dy), device_id_type=MESH)
 
-    def convolve(p, main, edges, dot, meanwhile):
-        val = inner[p]
-        for k, w in enumerate(WAYS):
-            if k == 4:
-                packed[p, 0] = pack(val[:, 0:128].astype(F32), 0)
-                packed[p, 1] = pack(val[:, LANES - 128 :].astype(F32), 3)
-
-            @pl.when(exists(w))
+    def send(p, start, stop):
+        for k in range(start, stop):
+            @pl.when(exists(WAYS[k]))
             def _(k=k):
                 halo(p, k).start()
+
+    def send_sides(p):
+        send(p, 0, 4)
+        packed[p, 0] = pack(inner[p, :, 0:128].astype(F32), 0)
+        packed[p, 1] = pack(inner[p, :, LANES - 128 :].astype(F32), 3)
+        send(p, 4, 6)
+
+    def convolve(p, main, edges, dot, meanwhile):
+        send(p, 6, 8)
+        val = inner[p]
         first = lax.broadcasted_iota(jnp.int32, (1, 128), 1) < C
 
         def seam(v):
@@ -319,9 +325,16 @@
         for tile_no in (1, 2):
             gate(tile_no, slice(SIDE, COLS - SIDE))
 
+    rest = sums[:, 0:HALF] + nt(hot[:, CAP:], masked[0:HALF, CAP:])
+    inner[0, :, 0:128] = (rest[:, 0:128] * div[:, 0:128]).astype(BF16)
+    inner[0, :, LANES - 128 :] = (rest[:, 128:] * div[:, LANES - 128 :]).astype(BF16)
+    send_sides(0)
+    rest = sums[:, HALF:] + nt(hot[:, CAP:], masked[HALF:LANES, CAP:])
+    inner[0, :, 128 : LANES - 128] = (rest * div[:, 128 : LANES - 128]).astype(BF16)
     convolve(0, forward, bef, nn, first_wait)
     for tile_no in (0, 3):
         gate(tile_no, slice(0, COLS))
+    send_sides(1)
     for tile_no in (1, 2):
         gate(tile_no, slice(0, SIDE))
         gate(tile_no, slice(COLS - SIDE, COLS))

time: 20.1 us -> 20.2 us (level)
  no operation moved by 1% of the time
where the time goes in v8:
time: 20.2 us; the launch traced here: 20.1 us
  Pallas kernels  19.4 us (96%)
  local copies, waits for them, and re-layouts  0.63 us (3%)
    pallas_call x1, Pallas kernels, per_device(): pl.pallas_call(functools.partial(kernel, n, ns), out_shape=pltpu.VMEM((C,...  19.4 us
    unnamed x1, local copies, waits for them, and re-layouts  0.63 us

profile of v8, /device:TPU:0, one launch (start us, length us, event | category | flops | bytes accessed | tf_op | source)
XLA Modules:
  0.0 20.1 jit_solution(6951173772964645042)
XLA Ops:
  0.0 19.4 %shard_map.46 = bf16[32,1024]{1,0:T(8,128)(2,1)S(1)} custom-call(bf16[32,1024]{1,0:T(8,128)(2,1)} %bitcast.7, bf16[32,1024]{1,0:T(8,128)(2,1)} %bitcast.8, s32[4,1,256]{2,1,0:T(1,128)} %bitcast.9, bf16[864,32]{1,0:T(8,128)(2,1)} %bitcast.6), custom_call_target="tpu_custom_call" | custom-call | tf_op jit(solution)/shard_map/pallas_call | solution.py:383
  19.4 0.6 %copy.6 = bf16[1024,32]{0,1:T(8,128)(2,1)} copy(bf16[1024,32]{0,1:T(8,128)(2,1)S(1)} %bitcast.5) | data formatting | bytes 131072

commit v9 on v7

--- a/solution.py
+++ b/solution.py
@@ -32,7 +32,7 @@
 
 def kernel(
     n, ns, feats, cots, vox, weights, out,
-    gotf, gotc, gotv, w_in, hot, masked, sums, tiled, bmf, bef, beb,
+    gotf, gotc, gotv, w_in, hot, masked, sums, tiled, bmf, bef,
     inner, packed, hx, hc, hy, xm, xe, xh, xf, acc, gy, div, back,
     local, fs, fr, cs, cr, vs, vr, hs, hr, rs, rr,
 ):
@@ -92,16 +92,15 @@
     xe[0:SIDE, :] = jnp.zeros((SIDE, 3 * 128), BF16)
     xe[COLS + SIDE : COLS + 2 * SIDE, :] = jnp.zeros((SIDE, 3 * 128), BF16)
 
-    for dy in range(3):
-        for dz in range(3):
-            for i in range(HALF // C):
-                for h in range(2):
-                    if (i, h) not in BANDS:
-                        bmf[dy, dz * HALF + i * C : dz * HALF + (i + 1) * C, h * 128 : (h + 1) * 128] = jnp.zeros(
-                            (C, 128), BF16)
-            bef[dy, dz * 128 : (dz + 1) * 128, :128] = jnp.zeros((128, 128), BF16)
-            bef[dy, dz * 128 : (dz + 1) * 128, 128:] = jnp.zeros((128, 128), BF16)
-            beb[dy, C : HALF - C, dz * 128 : (dz + 1) * 128] = jnp.zeros((HALF - 2 * C, 128), BF16)
+    for p in range(2):
+        for dy in range(3):
+            for dz in range(3):
+                for i in range(HALF // C):
+                    for h in range(2):
+                        if (i, h) not in BANDS:
+                            at = slice(dz * HALF + i * C, dz * HALF + (i + 1) * C)
+                            bmf[p, dy, at, h * 128 : (h + 1) * 128] = jnp.zeros((C, 128), BF16)
+            bef[p, dy] = jnp.zeros((3 * 128, HALF), BF16)
 
     peers = n - 1
     for w in outer:
@@ -135,27 +134,22 @@
     spread = jnp.where(
         (lax.broadcasted_iota(jnp.int32, (C, 128), 1) & (C - 1)) == lax.broadcasted_iota(jnp.int32, (C, 128), 0),
         1.0, 0.0).astype(BF16)
-    tiled[...] = nn(w_in[...], spread)
-
-    def tile(dx, dy, dz):
-        a = (dx * 3 + dy) * 3 + dz
-        return tiled[a * C : (a + 1) * C, :]
-
-    for dy in range(3):
-        for dz in range(3):
-            w0, w1, w2 = (tile(dx, dy, dz) for dx in range(3))
+    turned = jnp.swapaxes(w_in[...].astype(F32).reshape(27, C, C), 1, 2).reshape(27 * C, C).astype(BF16)
+    tiled[0] = nn(w_in[...], spread).reshape(27, C, 128)
+    tiled[1] = nn(turned, spread).reshape(27, C, 128)
+
+    for p in range(2):
+        for a in range(9):
+            dy, dz = a // 3, a % 3
+            w0, w1, w2 = (tiled[p, 26 - dx * 9 - a if p else dx * 9 + a] for dx in range(3))
             for i, h in BANDS:
                 piece = 0.0
                 for at, w in ((i + 1, w0), (i - 1, w2), (i, w1)):
                     if at // 4 == h:
                         piece = jnp.where(block == at % 4, w, piece)
-                bmf[dy, dz * HALF + i * C : dz * HALF + (i + 1) * C, h * 128 : (h + 1) * 128] = piece.astype(BF16)
-            high, low = jnp.where(block == 3, w2, 0.0).astype(BF16), jnp.where(block == 0, w0, 0.0).astype(BF16)
-            bef[dy, dz * 128 : dz * 128 + C, 128:] = high
-            bef[dy, dz * 128 + 3 * C : dz * 128 + 4 * C, :128] = low
-            at = slice((2 - dz) * 128, (3 - dz) * 128)
-            beb[2 - dy, HALF - C :, at] = low
-            beb[2 - dy, 0:C, at] = high
+                bmf[p, dy, dz * HALF + i * C : dz * HALF + (i + 1) * C, h * 128 : (h + 1) * 128] = piece.astype(BF16)
+            bef[p, dy, dz * 128 : dz * 128 + C, 128:] = jnp.where(block == 3, w2, 0.0).astype(BF16)
+            bef[p, dy, dz * 128 + 3 * C : dz * 128 + 4 * C, :128] = jnp.where(block == 0, w0, 0.0).astype(BF16)
 
     row = lax.broadcasted_iota(jnp.int32, (COLS, CAP), 0)
 
@@ -223,7 +217,13 @@
             src_ref=src, dst_ref=dst, send_sem=hs.at[p, k], recv_sem=hr.at[p, k],
             device_id=(s + dx, g + dy), device_id_type=MESH)
 
-    def convolve(p, main, edges, dot, meanwhile):
+    def convolve(p, meanwhile):
+        def main(lhs, dy):
+            return nn(lhs, bmf[p, dy])
+
+        def edged(lhs, dy):
+            return nn(lhs, bef[p, dy])
+
         val = inner[p]
         for k, w in enumerate(WAYS):
             if k == 4:
@@ -247,7 +247,7 @@
         def row_step(dy, first_step):
             at = pl.ds(pl.multiple_of(dy * SIDE, SIDE), COLS)
             term = main(xm[:, at, :].reshape(2 * COLS, 3 * HALF), dy).reshape(2, COLS, HALF)
-            inside = dot(xe[at, :], edges[dy])
+            inside = edged(xe[at, :], dy)
             if first_step:
                 acc[...] = term
             else:
@@ -280,9 +280,9 @@
             for b in range(2))
         for j, part in enumerate(shifts(jnp.where(first, right, left))):
             xf[SIDE : COLS + 3 * SIDE, j * 128 : (j + 1) * 128] = part
-        upper = dot(xf[0 : COLS + SIDE, :], edges[0])
-        lower = dot(xf[3 * SIDE : COLS + 4 * SIDE, :], edges[2])
-        total = upper[SIDE:] + dot(xf[2 * SIDE : COLS + 2 * SIDE, :], edges[1]) + lower[:COLS]
+        upper = edged(xf[0 : COLS + SIDE, :], 0)
+        lower = edged(xf[3 * SIDE : COLS + 4 * SIDE, :], 2)
+        total = upper[SIDE:] + edged(xf[2 * SIDE : COLS + 2 * SIDE, :], 1) + lower[:COLS]
         acc[0, :, :128] += total[:, :128]
         acc[1, :, 128:] += total[:, 128:]
         for side, dy, r0, rim in ((0, 0, 0, upper[:SIDE]), (1, 2, COLS - SIDE, lower[COLS:])):
@@ -299,17 +299,6 @@
         sig = 1.0 / (1.0 + jnp.exp(-o))
         inner[1, rows, at] = (gy[rows, at] * sig * (1.0 + o * (1.0 - sig))).astype(BF16)
 
-    def forward(lhs, dy):
-        return nn(lhs, bmf[dy])
-
-    def backward(lhs, dy):
-        total = None
-        for dz in range(3):
-            flip = slice((2 - dz) * HALF, (3 - dz) * HALF)
-            term = nt(lhs[:, dz * HALF : (dz + 1) * HALF], bmf[2 - dy, flip, :])
-            total = term if total is None else total + term
-        return total
-
     def first_wait():
         for d in range(n):
             if d:
@@ -319,13 +308,17 @@
         for tile_no in (1, 2):
             gate(tile_no, slice(SIDE, COLS - SIDE))
 
-    convolve(0, forward, bef, nn, first_wait)
-    for tile_no in (0, 3):
-        gate(tile_no, slice(0, COLS))
-    for tile_no in (1, 2):
-        gate(tile_no, slice(0, SIDE))
-        gate(tile_no, slice(COLS - SIDE, COLS))
-    convolve(1, backward, beb, nt, lambda: None)
+    def second_input():
+        for tile_no in (0, 3):
+            gate(tile_no, slice(0, COLS))
+        for tile_no in (1, 2):
+            gate(tile_no, slice(0, SIDE))
+            gate(tile_no, slice(COLS - SIDE, COLS))
+
+    @pl.loop(0, 2)
+    def _(p):
+        convolve(p, lambda: pl.when(p == 0)(first_wait))
+        pl.when(p == 0)(second_input)
 
     grad = jnp.concatenate([acc[b] * div[:, b * HALF : (b + 1) * HALF] for b in range(2)], axis=1)
     grad = jnp.transpose(grad).astype(BF16)
@@ -380,10 +373,9 @@
             vm((COLS, slots), BF16),
             vm((3 * LANES, slots), BF16),
             vm((COLS, LANES), F32),
-            vm((27 * C, 128), F32),
-            vm((3, 3 * HALF, HALF), BF16),
-            vm((3, 3 * 128, HALF), BF16),
-            vm((3, HALF, 3 * 128), BF16),
+            vm((2, 27, C, 128), F32),
+            vm((2, 3, 3 * HALF, HALF), BF16),
+            vm((2, 3, 3 * 128, HALF), BF16),
             vm((2, COLS, LANES), BF16),
             vm((2, 2, COLS // 4, 128), BF16),
             vm((2, 2, COLS // 4, 128), BF16),

time: 20.1 us -> 20 us (level)
  no operation moved by 1% of the time
where the time goes in v9:
time: 20 us; the launch traced here: 19.9 us
  Pallas kernels  19.3 us (96%)
  local copies, waits for them, and re-layouts  0.63 us (3%)
    pallas_call x1, Pallas kernels, per_device(): pl.pallas_call(functools.partial(kernel, n, ns), out_shape=pltpu.VMEM((C,...  19.3 us
    unnamed x1, local copies, waits for them, and re-layouts  0.63 us

profile of v9, /device:TPU:0, one launch (start us, length us, event | category | flops | bytes accessed | tf_op | source)
XLA Modules:
  0.0 19.9 jit_solution(18223985650486716027)
XLA Ops:
  0.0 19.3 %shard_map.46 = bf16[32,1024]{1,0:T(8,128)(2,1)S(1)} custom-call(bf16[32,1024]{1,0:T(8,128)(2,1)} %bitcast.7, bf16[32,1024]{1,0:T(8,128)(2,1)} %bitcast.8, s32[4,1,256]{2,1,0:T(1,128)} %bitcast.9, bf16[864,32]{1,0:T(8,128)(2,1)} %bitcast.6), custom_call_target="tpu_custom_call" | custom-call | tf_op jit(solution)/shard_map/pallas_call | solution.py:363
  19.3 0.6 %copy.6 = bf16[1024,32]{0,1:T(8,128)(2,1)} copy(bf16[1024,32]{0,1:T(8,128)(2,1)S(1)} %bitcast.5) | data formatting | bytes 131072

commit v10 on v7

--- a/solution.py
+++ b/solution.py
@@ -262,10 +262,13 @@
             row_step(dy, False)
 
         meanwhile()
-        for k, w in enumerate(WAYS):
-            @pl.when(exists((-w[0], -w[1])))
-            def _(k=k):
-                halo(p, k).wait_recv()
+        def arrived(start, stop):
+            for k in range(start, stop):
+                @pl.when(exists((-WAYS[k][0], -WAYS[k][1])))
+                def _(k=k):
+                    halo(p, k).wait_recv()
+
+        arrived(6, 8)
         for side in range(2):
             rim = hy[p, side]
             for b in range(2):
@@ -274,6 +277,10 @@
             for j, part in enumerate(shifts(seam(rim))):
                 r0 = side * (COLS + 3 * SIDE)
                 xf[r0 : r0 + SIDE, j * 128 : (j + 1) * 128] = part
+        for side, dy, r0 in ((0, 0, 0), (1, 2, COLS - SIDE)):
+            term = main(xh[side].reshape(2 * SIDE, 3 * HALF), dy)
+            acc[:, r0 : r0 + SIDE, :] += term.reshape(2, SIDE, HALF)
+        arrived(0, 6)
         left, right = (
             jnp.concatenate(
                 [hc[p, b, 0].astype(F32), unpack(hx[p, b], 0 if b else 3), hc[p, b, 1].astype(F32)], axis=0)
@@ -285,10 +292,8 @@
         total = upper[SIDE:] + dot(xf[2 * SIDE : COLS + 2 * SIDE, :], edges[1]) + lower[:COLS]
         acc[0, :, :128] += total[:, :128]
         acc[1, :, 128:] += total[:, 128:]
-        for side, dy, r0, rim in ((0, 0, 0, upper[:SIDE]), (1, 2, COLS - SIDE, lower[COLS:])):
+        for r0, rim in ((0, upper[:SIDE]), (COLS - SIDE, lower[COLS:])):
             at = slice(r0, r0 + SIDE)
-            term = main(xh[side].reshape(2 * SIDE, 3 * HALF), dy)
-            acc[:, at, :] += term.reshape(2, SIDE, HALF)
             acc[0, at, 128:] += rim[:, 128:]
             acc[1, at, :128] += rim[:, :128]
 

time: 20.1 us -> 19.9 us (0.990)
  no operation moved by 1% of the time
where the time goes in v10:
time: 19.9 us; the launch traced here: 19.7 us
  Pallas kernels  19.1 us (96%)
  local copies, waits for them, and re-layouts  0.63 us (3%)
    pallas_call x1, Pallas kernels, per_device(): pl.pallas_call(functools.partial(kernel, n, ns), out_shape=pltpu.VMEM((C,...  19.1 us
    unnamed x1, local copies, waits for them, and re-layouts  0.63 us

profile of v10, /device:TPU:0, one launch (start us, length us, event | category | flops | bytes accessed | tf_op | source)
XLA Modules:
  0.0 19.7 jit_solution(6581309162903502154)
XLA Ops:
  0.0 19.1 %shard_map.46 = bf16[32,1024]{1,0:T(8,128)(2,1)S(1)} custom-call(bf16[32,1024]{1,0:T(8,128)(2,1)} %bitcast.7, bf16[32,1024]{1,0:T(8,128)(2,1)} %bitcast.8, s32[4,1,256]{2,1,0:T(1,128)} %bitcast.9, bf16[864,32]{1,0:T(8,128)(2,1)} %bitcast.6), custom_call_target="tpu_custom_call" | custom-call | tf_op jit(solution)/shard_map/pallas_call | solution.py:375
  19.1 0.6 %copy.6 = bf16[1024,32]{0,1:T(8,128)(2,1)} copy(bf16[1024,32]{0,1:T(8,128)(2,1)S(1)} %bitcast.5) | data formatting | bytes 131072
